TPU v7x, 32 devices: a whole 2x2x4 slice. The times are simulated.
32 devices in a mesh: section: 4 (over x, core), sample: 2 (over y), tensor: 4 (over z).
Axes of the slice: x: 2, y: 2, z: 4, core: 2. Of those that a mesh axis runs over, the one named last changes fastest.
Arguments:
- queries: bfloat16 [4, 256, 8192], P('section', 'sample', 'tensor'), may hold values from -4.5 to 4.5
- suffix_keys: bfloat16 [4, 256, 1024], P('section', 'sample', 'tensor'), may hold values from -4.5 to 4.5
- suffix_values: bfloat16 [4, 256, 1024], P('section', 'sample', 'tensor'), may hold values from -4.5 to 4.5
- output_grad: bfloat16 [4, 256, 8192], P('section', 'sample', 'tensor'), may hold values from -192 to 192
- prefix_keys: bfloat16 [4, 1024, 1024], P('section', ('sample', 'tensor')), may hold values from -4.5 to 4.5
- prefix_values: bfloat16 [4, 1024, 1024], P('section', ('sample', 'tensor')), may hold values from -4.5 to 4.5
- kv_weight: bfloat16 [4, 8192, 2, 1024], P('section', None, None, 'tensor'), may hold values from -0.0625 to 0.0625
- prefix_states: bfloat16 [4, 1024, 8192], P('section', ('sample', 'tensor')), may hold values from -6 to 6
- norm_gain: bfloat16 [4, 8192], P('section'), may hold values from 0.099609375 to 1.8984375
- segment_ids: int32 [2, 128], P('sample'), may hold values from 0 to 1, never falling along the last dimension, each value on 1 to 96 neighbouring positions
- segment_prompt: int32 [2, 2], P('sample'), may hold values from 0 to 2
- block_table: int32 [3, 4], replicated, may hold values from 0 to 7, as said below
Outputs:
- query_grad: bfloat16 [4, 256, 8192], P('section', 'sample', 'tensor')
- rollout_key_gradient: bfloat16 [4, 256, 1024], P('section', 'sample', 'tensor')
- suffix_value_grad: bfloat16 [4, 256, 1024], P('section', 'sample', 'tensor')
- prefix_key_grad: float32 [4, 1024, 1024], P('section', ('sample', 'tensor'))
- prefix_value_grad: float32 [4, 1024, 1024], P('section', ('sample', 'tensor'))
- prefix_state_gradient: float32 [4, 1024, 8192], P('section', ('sample', 'tensor'))
Inputs may be any that keep to these rules, and one draw needn't show every extreme that they name: `block_table`: each row lists 4 distinct pages; its first 2 entries are the same pages in every row, and every page of the pool appears in some row.
All inputs are finite; a program needn't handle non-finite values.
Results may differ from a plain program's by a relative error of at most 0.024.
Values may be sent and summed in bfloat16 or wider, within the bound.
A program may use at most 192 MiB of HBM per device.

v0:
```python
import jax
import jax.numpy as jnp
from jax import lax
from jax.sharding import PartitionSpec as P

HEAD_SIZE = 128
PAGE = 128


MASKED_SCORE = -1e30
EPSILON = 1e-05
CHUNKS = 4
AHEAD = 2


def visible_keys(seg_row, prompt_row, table, page_ids):
    tok_count = seg_row.shape[0]
    seg_hot = seg_row[:, None] == jnp.arange(prompt_row.shape[0], dtype=jnp.int32)[None, :]
    prompt_tok = jnp.sum(jnp.where(seg_hot, prompt_row[None, :], 0), axis=1)
    member = jnp.any(table[:, :, None] == page_ids[None, None, :], axis=1)
    prompt_hot = prompt_tok[:, None] == jnp.arange(table.shape[0], dtype=jnp.int32)[None, :]
    member_tok = jnp.any(prompt_hot[:, :, None] & member[None, :, :], axis=1)
    prefix_seen = jnp.repeat(member_tok, PAGE, axis=1)
    position = jnp.arange(tok_count, dtype=jnp.int32)
    suffix_seen = (seg_row[:, None] == seg_row[None, :]) & (position[None, :] <= position[:, None])
    return jnp.concatenate([prefix_seen, suffix_seen], axis=1)


def attend_group(query_grp, grad_grp, key_rows, value_rows, visible):
    inv_root = query_grp.shape[-1] ** (-0.5)
    scores = (
        jnp.einsum("rgd,kd->rgk", query_grp, key_rows, preferred_element_type=jnp.float32)
        * inv_root
    )
    scores = jnp.where(visible[:, None, :], scores, MASKED_SCORE)
    row_max = jnp.max(scores, axis=2, keepdims=True)
    exponent = jnp.exp(scores - row_max)
    softmax_w = exponent / jnp.sum(exponent, axis=2, keepdims=True)
    weights_low = softmax_w.astype(jnp.bfloat16)
    attended = jnp.einsum(
        "rgk,kd->rgd", weights_low, value_rows, preferred_element_type=jnp.float32
    )
    delta_row = jnp.sum(grad_grp.astype(jnp.float32) * attended, axis=2, keepdims=True)
    weight_grad = jnp.einsum(
        "rgd,kd->rgk", grad_grp, value_rows, preferred_element_type=jnp.float32
    )
    score_grad = (softmax_w * (weight_grad - delta_row)).astype(jnp.bfloat16)
    query_out = (
        jnp.einsum("rgk,kd->rgd", score_grad, key_rows, preferred_element_type=jnp.float32)
        * inv_root
    )
    key_result = (
        jnp.einsum("rgk,rgd->kd", score_grad, query_grp, preferred_element_type=jnp.float32)
        * inv_root
    )
    value_out = jnp.einsum("rgk,rgd->kd", weights_low, grad_grp, preferred_element_type=jnp.float32)
    return (query_out, key_result, value_out)


def swap(value, axis, bit):
    count = lax.axis_size(axis)
    return lax.ppermute(value, axis, [(i, i ^ bit) for i in range(count)])


def sample_gather(value, axis):
    if lax.axis_size("sample") == 2:
        return jnp.concatenate([value, swap(value, "sample", 1)], axis=axis)
    return lax.all_gather(value, "sample", axis=axis, tiled=True)


def sample_reduce(value):
    count = lax.axis_size("sample")
    rows = value.shape[0] // count
    if count == 2:
        theirs = swap(value[rows:].astype(jnp.bfloat16), "sample", 1)
        return value[:rows] + theirs.astype(jnp.float32)
    low = value.astype(jnp.bfloat16)
    return lax.psum_scatter(low, "sample", scatter_dimension=0, tiled=True).astype(jnp.float32)


def times_weight(rows, weight):
    last = rows.ndim - 1
    return lax.dot_general(
        rows, weight, (((last - 1, last), (1, 2)), ((), ())), preferred_element_type=jnp.float32
    )


def tied(*values):
    return lax.optimization_barrier(values)


def suffix_sum(term):
    count = lax.axis_size("section")
    place = lax.axis_index("section")
    low = term.astype(jnp.bfloat16)
    if count != 4:
        gathered = lax.all_gather(low, "section").astype(jnp.float32)
        above = (jnp.arange(count) > place)[:, None, None]
        return term + jnp.sum(jnp.where(above, gathered, 0.0), axis=0)
    odd = place % 2 == 1
    half = term.shape[1] // 2
    peer = swap(low, "section", 1).astype(jnp.float32)
    pair = (term + peer).astype(jnp.bfloat16)
    part = jnp.where(odd, pair[:, half:], pair[:, :half])
    got = lax.ppermute(part, "section", [(2, 0), (3, 1)])
    other = lax.ppermute(got, "section", [(0, 1), (1, 0)])
    upper = jnp.where(
        odd, jnp.concatenate([other, got], axis=1), jnp.concatenate([got, other], axis=1)
    )
    return term + jnp.where(odd, 0.0, peer) + upper.astype(jnp.float32)


def from_above(value, step):
    count = lax.axis_size("section")
    return lax.ppermute(value, "section", [(i, i - step) for i in range(step, count)])


def on_device(
    queries,
    suffix_keys,
    suffix_values,
    output_grad,
    prefix_keys,
    prefix_values,
    kv_weight,
    prefix_states,
    norm_gain,
    segment_ids,
    segment_prompt,
    block_table,
):
    head_width = suffix_keys.shape[2]
    samples = lax.axis_size("sample")
    sample = lax.axis_index("sample")
    tensors = lax.axis_size("tensor")
    tensor = lax.axis_index("tensor")
    sections = lax.axis_size("section")

    pool_own = jnp.concatenate([prefix_keys, prefix_values], axis=0)
    pool_mine = lax.all_to_all(pool_own, "tensor", split_axis=2, concat_axis=1, tiled=True)
    pool = sample_gather(pool_mine, 1)
    key_pool, value_pool = pool[0], pool[1]
    pooled_rows = key_pool.shape[0]
    pages = pooled_rows // PAGE
    page_ids = jnp.arange(pages, dtype=jnp.int32)
    if samples == 2:
        page_ids = (page_ids + sample.astype(jnp.int32) * (pages // 2)) % pages

    weight = kv_weight[0]
    width = weight.shape[0]
    step = width // CHUNKS
    piece = step // samples
    partner_half = []
    for chunk in range(AHEAD):
        mine = lax.dynamic_slice_in_dim(weight, chunk * step + sample * piece, piece, 0)
        partner_half.append(swap(mine, "tensor", 1))

    states_low = prefix_states[0]
    if sections == 4:
        states_across = [lax.ppermute(states_low, "section", [(2, 0), (3, 1)])]
    else:
        states_across = [from_above(states_low, hop) for hop in range(1, sections)]

    tok_count = queries.shape[1]
    kv_local = head_width // HEAD_SIZE
    group_size = queries.shape[2] // head_width
    visible = visible_keys(segment_ids[0], segment_prompt[0], block_table, page_ids)
    query_rows = queries[0].reshape(tok_count, kv_local, group_size, HEAD_SIZE)
    grad_rows = output_grad[0].reshape(tok_count, kv_local, group_size, HEAD_SIZE)
    own_keys = suffix_keys[0]
    own_values = suffix_values[0]
    query_pieces, suffix_key_pieces, suffix_value_pieces, prefix_key_pieces, prefix_value_pieces = (
        [],
        [],
        [],
        [],
        [],
    )
    for head_index in range(kv_local):
        low_col = head_index * HEAD_SIZE
        cols = slice(low_col, low_col + HEAD_SIZE)
        if head_index == 1:
            key_pool, value_pool, partner_half, states_across = tied(
                key_pool, value_pool, partner_half, states_across
            )
        key_rows = jnp.concatenate([key_pool[:, cols], own_keys[:, cols]], axis=0)
        value_rows = jnp.concatenate([value_pool[:, cols], own_values[:, cols]], axis=0)
        query_out, key_result, value_out = attend_group(
            query_rows[:, head_index], grad_rows[:, head_index], key_rows, value_rows, visible
        )
        query_pieces.append(query_out)
        prefix_key_pieces.append(key_result[:pooled_rows])
        suffix_key_pieces.append(key_result[pooled_rows:])
        prefix_value_pieces.append(value_out[:pooled_rows])
        suffix_value_pieces.append(value_out[pooled_rows:])
    query_grad = jnp.stack(query_pieces, axis=1).reshape(tok_count, -1).astype(jnp.bfloat16)
    rollout_key_gradient = jnp.concatenate(suffix_key_pieces, axis=1).astype(jnp.bfloat16)
    suffix_value_grad = jnp.concatenate(suffix_value_pieces, axis=1).astype(jnp.bfloat16)
    pooled = jnp.concatenate(prefix_key_pieces + prefix_value_pieces, axis=1)
    reduced = sample_reduce(pooled).astype(jnp.bfloat16)

    partner_weight = [sample_gather(half, 0) for half in partner_half]
    if sections == 4:
        states_above = [
            swap(states_low, "section", 1),
            states_across[0],
            swap(states_across[0], "section", 1),
        ]
    else:
        states_above = states_across
    reduced, partner_weight, states_above = tied(reduced, partner_weight, states_above)

    own_rows = reduced.shape[0] // tensors
    high, low = tensor // 2, tensor % 2
    by_owner = reduced.reshape(tensors // 2, 2, own_rows, 2, head_width)
    keep = lax.dynamic_index_in_dim(by_owner, low, 1, False)
    give = lax.dynamic_index_in_dim(by_owner, 1 - low, 1, False)
    partner = swap(give, "tensor", 1)
    here = lambda rows: lax.dynamic_index_in_dim(rows, high, 0, False)
    there = lambda rows: lax.dynamic_index_in_dim(rows, 1 - high, 0, False)

    gain_wide = norm_gain[0].astype(jnp.float32)[None, :]
    states = states_low.astype(jnp.float32)
    inv_rms = lax.rsqrt(jnp.mean(states * states, axis=1, keepdims=True) + EPSILON)

    def partner_product(rows, chunk):
        pieces = times_weight(rows, partner_weight[chunk])
        if samples != 2:
            return pieces
        turned = jnp.concatenate([pieces[..., piece:], pieces[..., :piece]], axis=-1)
        return jnp.where(sample == 0, pieces, turned)

    owns = [weight[chunk * step : (chunk + 1) * step] for chunk in range(CHUNKS)]
    local, sent, theirs = {}, {}, {}
    for chunk in range(AHEAD, CHUNKS):
        theirs[chunk] = swap(
            times_weight(give, owns[chunk]).astype(jnp.bfloat16), "tensor", 1
        )
    for chunk in range(AHEAD):
        total = times_weight(keep, owns[chunk]) + partner_product(partner, chunk)
        sent[chunk] = swap(there(total).astype(jnp.bfloat16), "tensor", 2)
        local[chunk] = here(total)
    for chunk in range(AHEAD, CHUNKS):
        total = times_weight(keep, owns[chunk]) + theirs[chunk].astype(jnp.float32)
        sent[chunk] = swap(there(total).astype(jnp.bfloat16), "tensor", 2)
        local[chunk] = here(total)

    home = lax.all_to_all(
        reduced.reshape(-1, 2, head_width), "tensor", split_axis=0, concat_axis=2, tiled=True
    ).astype(jnp.float32)
    last = CHUNKS - 1
    sent[last], home, query_grad, rollout_key_gradient, suffix_value_grad = tied(
        sent[last], home, query_grad, rollout_key_gradient, suffix_value_grad
    )

    sums, along = [], 0.0
    for chunk in range(CHUNKS):
        cols = slice(chunk * step, (chunk + 1) * step)
        normed = local[chunk] + sent[chunk].astype(jnp.float32)
        gained = gain_wide[:, cols] * normed
        along = along + jnp.sum(states[:, cols] * gained, axis=1)
        sums.append(suffix_sum(inv_rms * gained))
    slope = inv_rms[:, 0] ** 3 * (along / width)
    state_part = states * slope[:, None]
    if sections == 4:
        peer = swap(slope, "section", 1)
        across = lax.ppermute(slope, "section", [(2, 0), (3, 1)])
        across_peer = lax.ppermute(slope, "section", [(2, 1), (3, 0)])
        odd = lax.axis_index("section") % 2 == 1
        slopes_above = [jnp.where(odd, 0.0, peer), across, across_peer]
    else:
        slopes_above = [from_above(slope, hop) for hop in range(1, sections)]
    for above, slope_above in zip(states_above, slopes_above):
        state_part = state_part + above.astype(jnp.float32) * slope_above[:, None]
    prefix_state_gradient = jnp.concatenate(sums, axis=1) - state_part

    return (
        query_grad[None],
        rollout_key_gradient[None],
        suffix_value_grad[None],
        home[:, 0][None],
        home[:, 1][None],
        prefix_state_gradient[None],
    )


def solution(mesh):
    placed = (
        P("section", "sample", "tensor"),
        P("section", "sample", "tensor"),
        P("section", "sample", "tensor"),
        P("section", "sample", "tensor"),
        P("section", ("sample", "tensor"), None),
        P("section", ("sample", "tensor"), None),
        P("section", None, None, "tensor"),
        P("section", ("sample", "tensor"), None),
        P("section", None),
        P("sample", None),
        P("sample", None),
        P(),
    )
    return jax.shard_map(
        on_device,
        mesh=mesh,
        in_specs=placed,
        out_specs=(
            P("section", "sample", "tensor"),
            P("section", "sample", "tensor"),
            P("section", "sample", "tensor"),
            P("section", ("sample", "tensor"), None),
            P("section", ("sample", "tensor"), None),
            P("section", ("sample", "tensor"), None),
        ),
        check_vma=False,
    )
```

profile of v0, /device:TPU:0, one launch (start us, length us, event | category | flops | bytes accessed | tf_op | source)
XLA Modules:
  0.0 343.7 jit_solution(15039634780605334721)
XLA Ops:
  4.6 5.9 %all-to-all-start = ((bf16[2,128,1024]{1,0,2:T(2,128)(2,1)}), bf16[2,128,1024]{1,0,2:T(2,128)(2,1)S(1)}, u32[]{:S(2)}, u32[]{:S(2)}) async-start(bf16[2,128,1024]{1,0,2:T(2,128)(2,1)} %copy.163), calls=%async_computation | async-start | bytes 1048576 | tf_op jit(solution)/shard_map/all_to_all | solution.py:140
  10.5 3.0 constant_dynamic-slice_fusion.2
  17.8 2.4 bitcast_convert_fusion
  24.1 9.3 %fusion.91 = (bf16[1,2048,2,256]{3,2,1,0:T(2,128)(2,1)}, bf16[1,2048,2,256]{3,2,1,0:T(2,128)(2,1)}, bf16[1,2048,2,256]{3,2,1,0:T(2,128)(2,1)}, bf16[1,2048,2,256]{3,2,1,0:T(2,128)(2,1)}) fusion(bf16[1,8192,2,256]{3,2,1,0:T(2,128)(2,1)} %param.18), kind=kLoop, calls=%fused_computation.203 | loop fusion | bytes 16777216 | tf_op jit(solution)/shard_map/slice | solution.py:233
  42.2 6.3 %collective-permute-done = bf16[2,512,256]{2,1,0:T(8,128)(2,1)} collective-permute-done((bf16[2,512,256]{2,1,0:T(8,128)(2,1)}, bf16[2,512,256]{2,1,0:T(8,128)(2,1)}, u32[]{:S(2)}, u32[]{:S(2)}) %collective-permute-start) | collective-permute-done | bytes 524320 | tf_op jit(solution)/shard_map/ppermute | solution.py:62
  50.6 4.8 %exponential_reduce_fusion.1 = (f32[128,8]{0,1:T(8,128)S(1)}, f32[128,8,1152]{0,2,1:T(8,128)}) fusion(pred[128,1152]{0,1:T(8,128)(4,1)} %pad_add_fusion, bf16[128,2,8,128]{0,3,2,1:T(8,128)(2,1)} %bitcast.314, bf16[128,128]{1,0:T(8,128)(2,1)} %get-tuple-element.96, bf16[1024,128]{1,0:T(8,128)(2,1)S(1)} %slice.223), kind=kOutput, calls=%fused_computation.19 | convolution fusion | flops 307299456 | bytes 5427200 | tf_op jit(solution)/shard_map/sub | solution.py:37
  55.5 3.1 fusion.21
  63.7 3.3 collective-permute-done.2
  69.2 4.8 %exponential_reduce_fusion = (f32[128,8]{0,1:T(8,128)S(1)}, f32[128,8,1152]{0,2,1:T(8,128)}) fusion(pred[128,1152]{0,1:T(8,128)(4,1)} %pad_add_fusion, bf16[128,2,8,128]{0,3,2,1:T(8,128)(2,1)} %bitcast.315, bf16[128,128]{1,0:T(8,128)(2,1)S(1)} %copy-done.56, bf16[1024,128]{1,0:T(8,128)(2,1)S(1)} %slice.176), kind=kOutput, calls=%fused_computation.17 | convolution fusion | flops 307299456 | bytes 5427200 | tf_op jit(solution)/shard_map/sub | solution.py:37
  74.0 3.1 fusion.22
  90.0 2.9 fusion.28
  92.9 32.7 %collective-permute-done.4 = bf16[512,512]{0,1:T(8,128)(2,1)} collective-permute-done((bf16[512,512]{0,1:T(8,128)(2,1)}, bf16[512,512]{0,1:T(8,128)(2,1)}, u32[]{:S(2)}, u32[]{:S(2)}) %collective-permute-start.4) | collective-permute-done | bytes 524320 | tf_op jit(solution)/shard_map/ppermute | solution.py:62
  126.8 3.0 pad_maximum_fusion.1
  129.8 3.0 pad_maximum_fusion.2
  134.1 4.1 %all-to-all-start.1 = ((bf16[512,2,256]{2,1,0:T(2,128)(2,1)}), bf16[512,2,256]{2,1,0:T(2,128)(2,1)}, u32[]{:S(2)}, u32[]{:S(2)}) async-start(bf16[512,2,256]{2,1,0:T(2,128)(2,1)} %copy.190), calls=%async_computation.1 | async-start | bytes 1048576 | tf_op jit(solution)/shard_map/all_to_all | solution.py:248
  144.9 2.3 fusion.10
  150.2 4.5 %collective-permute-done.11 = bf16[2,128,2,256]{3,1,2,0:T(8,128)(2,1)S(1)} collective-permute-done((bf16[2,128,2,256]{3,1,2,0:T(8,128)(2,1)S(1)}, bf16[2,128,2,256]{3,1,2,0:T(8,128)(2,1)S(1)}, u32[]{:S(2)}, u32[]{:S(2)}) %collective-permute-start.11) | collective-permute-done | bytes 262176 | tf_op jit(solution)/shard_map/ppermute | solution.py:62
  158.8 3.8 %collective-permute-start.16 = (bf16[128,2048]{1,0:T(8,128)(2,1)}, bf16[128,2048]{1,0:T(8,128)(2,1)S(1)}, u32[]{:S(2)}, u32[]{:S(2)}) collective-permute-start(bf16[128,2048]{1,0:T(8,128)(2,1)} %fusion.52), channel_id=1, source_target_pairs={{0,2},{1,3},{2,0},{3,1},{4,6},{5,7},{6,4},{7,5},{8,10},{9,11},{10,... | collective-permute-start | bytes 1572872 | tf_op jit(solution)/shard_map/ppermute | solution.py:62
  166.8 32.8 %collective-permute-done.20 = bf16[2,128,2048]{2,1,0:T(8,128)(2,1)S(1)} collective-permute-done((bf16[2,128,2048]{2,1,0:T(8,128)(2,1)S(1)}, bf16[2,128,2048]{2,1,0:T(8,128)(2,1)S(1)}, u32[]{:S(2)}, u32[]{:S(2)}) %collective-permute-start.20) | collective-permute-done | bytes 1048608 | tf_op jit(solution)/shard_map/ppermute | solution.py:62
  201.5 20.1 %collective-permute-done.9 = bf16[2,128,2048]{2,1,0:T(8,128)(2,1)S(1)} collective-permute-done((bf16[2,128,2048]{2,1,0:T(8,128)(2,1)S(1)}, bf16[2,128,2048]{2,1,0:T(8,128)(2,1)S(1)}, u32[]{:S(2)}, u32[]{:S(2)}) %collective-permute-start.9) | collective-permute-done | bytes 1048608 | tf_op jit(solution)/shard_map/ppermute | solution.py:62
  223.6 33.0 %collective-permute-done.21 = bf16[128,2048]{1,0:T(8,128)(2,1)S(1)} collective-permute-done((bf16[128,2048]{1,0:T(8,128)(2,1)S(1)}, bf16[128,2048]{1,0:T(8,128)(2,1)S(1)}, u32[]{:S(2)}, u32[]{:S(2)}) %collective-permute-start.21) | collective-permute-done | bytes 524320 | tf_op jit(solution)/shard_map/ppermute | solution.py:62
  263.9 2.7 reshape.114
  267.8 5.3 %fusion.43 = (f32[128]{0:T(128)S(1)}, f32[128]{0:T(128)S(1)}, f32[128]{0:T(128)S(1)}, f32[128]{0:T(128)S(1)}, bf16[128,2048]{1,0:T(8,128)(2,1)S(1)}, /*index=5*/...) fusion(f32[128,8192]{1,0:T(8,128)} %bitcast_convert_fusion, ...), kind=kLoop, calls=%fused_computation.95 | loop fusion | flops 7863808 | bytes 13142532 | tf_op jit(solution)/shard_map/reduce_sum | solution.py:261
  274.6 10.3 %collective-permute-done.23 = bf16[128,1024]{1,0:T(8,128)(2,1)S(1)} collective-permute-done((bf16[128,1024]{1,0:T(8,128)(2,1)S(1)}, bf16[128,1024]{1,0:T(8,128)(2,1)S(1)}, u32[]{:S(2)}, u32[]{:S(2)}) %collective-permute-start.23) | collective-permute-done | bytes 262176 | tf_op jit(solution)/shard_map/ppermute | solution.py:105
  284.9 2.2 collective-permute-start.24
  288.3 3.0 fusion.31
  293.2 8.7 %collective-permute-done.14 = bf16[128,1024]{1,0:T(8,128)(2,1)S(1)} collective-permute-done((bf16[128,1024]{1,0:T(8,128)(2,1)S(1)}, bf16[128,1024]{1,0:T(8,128)(2,1)S(1)}, u32[]{:S(2)}, u32[]{:S(2)}) %collective-permute-start.14) | collective-permute-done | bytes 262176 | tf_op jit(solution)/shard_map/ppermute | solution.py:105
  305.3 3.2 fusion.30
  312.5 7.4 %collective-permute-done.18 = bf16[128,1024]{1,0:T(8,128)(2,1)S(1)} collective-permute-done((bf16[128,1024]{1,0:T(8,128)(2,1)S(1)}, bf16[128,1024]{1,0:T(8,128)(2,1)S(1)}, u32[]{:S(2)}, u32[]{:S(2)}) %collective-permute-start.18) | collective-permute-done | bytes 262176 | tf_op jit(solution)/shard_map/ppermute | solution.py:105
  321.7 3.0 collective-permute-done.26
  334.5 3.4 fusion.33
  338.1 5.2 %fusion.8 = f32[1,128,8192]{2,1,0:T(8,128)} fusion(f32[128,2048]{1,0:T(8,128)S(1)} %get-tuple-element.108, f32[128,2048]{1,0:T(8,128)S(1)} %copy-done.27, f32[128,2048]{1,0:T(8,128)S(1)} %get-tuple-element.107, f32[128,2048]{1,0:T(8,128)S(1)} %copy-done.29, bf16[128,8192]{1,0:T(8,128)(2,1)} %collective-permute-done.8, ...), kind=kLoop, calls=%fused_computation.21 | loop fusion | flops 15728640 | bytes 16779264 | tf_op jit(solution)/shard_map/broadcast_in_dim | solution.py:283
  (266 shorter events, 98.6 us)
Async XLA Ops:
  0.6 132.2 %collective-permute-start.7 = (bf16[128,8192]{1,0:T(8,128)(2,1)}, bf16[128,8192]{1,0:T(8,128)(2,1)}, u32[]{:S(2)}, u32[]{:S(2)}) collective-permute-start(bf16[128,8192]{1,0:T(8,128)(2,1)} %bitcast.302), channel_id=1, source_target_pairs={{0,8},{8,0},{16,24},{24,16},{1,9},{9,1},{17,25},{25,17},{2,10},{10... | collective-permute-start | bytes 6291464 | tf_op jit(solution)/shard_map/ppermute | solution.py:62
  1.1 65.9 %collective-permute-start.3 = (bf16[128,8192]{1,0:T(8,128)(2,1)}, bf16[128,8192]{1,0:T(8,128)(2,1)}, u32[]{:S(2)}, u32[]{:S(2)}) collective-permute-start(bf16[128,8192]{1,0:T(8,128)(2,1)} %bitcast.303), channel_id=1, source_target_pairs={{16,0},{24,8},{17,1},{25,9},{18,2},{26,10},{19,3},{27,11},{20,4},{... | collective-permute-start | bytes 6291464 | tf_op jit(solution)/shard_map/ppermute | solution.py:160
  4.6 28.8 %all-to-all-start = ((bf16[2,128,1024]{1,0,2:T(2,128)(2,1)}), bf16[2,128,1024]{1,0,2:T(2,128)(2,1)S(1)}, u32[]{:S(2)}, u32[]{:S(2)}) async-start(bf16[2,128,1024]{1,0,2:T(2,128)(2,1)} %copy.163), calls=%async_computation | async-start | bytes 1048576 | tf_op jit(solution)/shard_map/all_to_all | solution.py:140
  14.7 49.0 %collective-permute-start.1 = (bf16[1024,2,256]{2,0,1:T(8,128)(2,1)}, bf16[1024,2,256]{2,0,1:T(8,128)(2,1)}, u32[]{:S(2)}, u32[]{:S(2)}) collective-permute-start(bf16[1024,2,256]{2,0,1:T(8,128)(2,1)} %bitcast.301), channel_id=1, source_target_pairs={{0,1},{1,0},{2,3},{3,2},{4,5},{5,4},{6,7},{7,6},{8,9},{9,8},{10,11... | collective-permute-start | bytes 3145736 | tf_op jit(solution)/shard_map/ppermute | solution.py:62
  17.8 49.2 %collective-permute-start.2 = (bf16[1024,2,256]{2,0,1:T(8,128)(2,1)}, bf16[1024,2,256]{2,0,1:T(8,128)(2,1)}, u32[]{:S(2)}, u32[]{:S(2)}) collective-permute-start(bf16[1024,2,256]{2,0,1:T(8,128)(2,1)} %bitcast.300), channel_id=1, source_target_pairs={{0,1},{1,0},{2,3},{3,2},{4,5},{5,4},{6,7},{7,6},{8,9},{9,8},{10,11... | collective-permute-start | bytes 3145736 | tf_op jit(solution)/shard_map/ppermute | solution.py:62
  34.7 13.9 %collective-permute-start = (bf16[2,512,256]{2,1,0:T(8,128)(2,1)}, bf16[2,512,256]{2,1,0:T(8,128)(2,1)}, u32[]{:S(2)}, u32[]{:S(2)}) collective-permute-start(bf16[2,512,256]{2,1,0:T(8,128)(2,1)} %bitcast.312), channel_id=1, source_target_pairs={{0,4},{4,0},{1,5},{5,1},{2,6},{6,2},{3,7},{7,3},{8,12},{12,8},{9,1... | collective-permute-start | bytes 1572872 | tf_op jit(solution)/shard_map/ppermute | solution.py:62
  67.1 59.7 %collective-permute-start.5 = (bf16[1024,2,256]{2,0,1:T(8,128)(2,1)}, bf16[1024,2,256]{2,0,1:T(8,128)(2,1)}, u32[]{:S(2)}, u32[]{:S(2)}) collective-permute-start(bf16[1024,2,256]{2,0,1:T(8,128)(2,1)} %collective-permute-done.1), channel_id=1, source_target_pairs={{0,4},{4,0},{1,5},{5,1},{2,6},{6,2},{3,7},{7,3},{8,12},{12,8},{9,1... | collective-permute-start | bytes 3145736 | tf_op jit(solution)/shard_map/ppermute | solution.py:62
  68.7 61.2 %collective-permute-start.6 = (bf16[1024,2,256]{2,0,1:T(8,128)(2,1)}, bf16[1024,2,256]{2,0,1:T(8,128)(2,1)}, u32[]{:S(2)}, u32[]{:S(2)}) collective-permute-start(bf16[1024,2,256]{2,0,1:T(8,128)(2,1)} %collective-permute-done.2), channel_id=1, source_target_pairs={{0,4},{4,0},{1,5},{5,1},{2,6},{6,2},{3,7},{7,3},{8,12},{12,8},{9,1... | collective-permute-start | bytes 3145736 | tf_op jit(solution)/shard_map/ppermute | solution.py:62
  69.2 63.7 %collective-permute-start.8 = (bf16[128,8192]{1,0:T(8,128)(2,1)}, bf16[128,8192]{1,0:T(8,128)(2,1)}, u32[]{:S(2)}, u32[]{:S(2)}) collective-permute-start(bf16[128,8192]{1,0:T(8,128)(2,1)} %collective-permute-done.3), channel_id=1, source_target_pairs={{0,8},{8,0},{16,24},{24,16},{1,9},{9,1},{17,25},{25,17},{2,10},{10... | collective-permute-start | bytes 6291464 | tf_op jit(solution)/shard_map/ppermute | solution.py:62
  85.0 40.6 %collective-permute-start.4 = (bf16[512,512]{0,1:T(8,128)(2,1)}, bf16[512,512]{0,1:T(8,128)(2,1)}, u32[]{:S(2)}, u32[]{:S(2)}) collective-permute-start(bf16[512,512]{0,1:T(8,128)(2,1)} %slice.331), channel_id=1, source_target_pairs={{0,4},{4,0},{1,5},{5,1},{2,6},{6,2},{3,7},{7,3},{8,12},{12,8},{9,1... | collective-permute-start | bytes 1572872 | tf_op jit(solution)/shard_map/ppermute | solution.py:62
  134.1 126.7 %all-to-all-start.1 = ((bf16[512,2,256]{2,1,0:T(2,128)(2,1)}), bf16[512,2,256]{2,1,0:T(2,128)(2,1)}, u32[]{:S(2)}, u32[]{:S(2)}) async-start(bf16[512,2,256]{2,1,0:T(2,128)(2,1)} %copy.190), calls=%async_computation.1 | async-start | bytes 1048576 | tf_op jit(solution)/shard_map/all_to_all | solution.py:248
  142.8 11.9 %collective-permute-start.11 = (bf16[2,128,2,256]{3,1,2,0:T(8,128)(2,1)S(1)}, bf16[2,128,2,256]{3,1,2,0:T(8,128)(2,1)S(1)}, u32[]{:S(2)}, u32[]{:S(2)}) collective-permute-start(bf16[2,128,2,256]{3,1,2,0:T(8,128)(2,1)S(1)} %bitcast.320), channel_id=1, source_target_pairs={{0,1},{1,0},{2,3},{3,2},{4,5},{5,4},{6,7},{7,6},{8,9},{9,8},{10,11... | collective-permute-start | bytes 786440 | tf_op jit(solution)/shard_map/ppermute | solution.py:62
  147.2 52.4 %collective-permute-start.20 = (bf16[2,128,2048]{2,1,0:T(8,128)(2,1)S(1)}, bf16[2,128,2048]{2,1,0:T(8,128)(2,1)S(1)}, u32[]{:S(2)}, u32[]{:S(2)}) collective-permute-start(bf16[2,128,2048]{2,1,0:T(8,128)(2,1)S(1)} %fusion.10), channel_id=1, source_target_pairs={{0,1},{1,0},{2,3},{3,2},{4,5},{5,4},{6,7},{7,6},{8,9},{9,8},{10,11... | collective-permute-start | bytes 3145736 | tf_op jit(solution)/shard_map/ppermute | solution.py:62
  148.2 73.3 %collective-permute-start.9 = (bf16[2,128,2048]{2,1,0:T(8,128)(2,1)S(1)}, bf16[2,128,2048]{2,1,0:T(8,128)(2,1)S(1)}, u32[]{:S(2)}, u32[]{:S(2)}) collective-permute-start(bf16[2,128,2048]{2,1,0:T(8,128)(2,1)S(1)} %fusion.9), channel_id=1, source_target_pairs={{0,1},{1,0},{2,3},{3,2},{4,5},{5,4},{6,7},{7,6},{8,9},{9,8},{10,11... | collective-permute-start | bytes 3145736 | tf_op jit(solution)/shard_map/ppermute | solution.py:62
  158.8 108.9 %collective-permute-start.16 = (bf16[128,2048]{1,0:T(8,128)(2,1)}, bf16[128,2048]{1,0:T(8,128)(2,1)S(1)}, u32[]{:S(2)}, u32[]{:S(2)}) collective-permute-start(bf16[128,2048]{1,0:T(8,128)(2,1)} %fusion.52), channel_id=1, source_target_pairs={{0,2},{1,3},{2,0},{3,1},{4,6},{5,7},{6,4},{7,5},{8,10},{9,11},{10,... | collective-permute-start | bytes 1572872 | tf_op jit(solution)/shard_map/ppermute | solution.py:62
  166.8 100.9 %collective-permute-start.12 = (bf16[128,2048]{1,0:T(8,128)(2,1)}, bf16[128,2048]{1,0:T(8,128)(2,1)}, u32[]{:S(2)}, u32[]{:S(2)}) collective-permute-start(bf16[128,2048]{1,0:T(8,128)(2,1)} %fusion.51), channel_id=1, source_target_pairs={{0,2},{1,3},{2,0},{3,1},{4,6},{5,7},{6,4},{7,5},{8,10},{9,11},{10,... | collective-permute-start | bytes 1572872 | tf_op jit(solution)/shard_map/ppermute | solution.py:62
  200.5 56.1 %collective-permute-start.21 = (bf16[128,2048]{1,0:T(8,128)(2,1)S(1)}, bf16[128,2048]{1,0:T(8,128)(2,1)S(1)}, u32[]{:S(2)}, u32[]{:S(2)}) collective-permute-start(bf16[128,2048]{1,0:T(8,128)(2,1)S(1)} %fusion.53), channel_id=1, source_target_pairs={{0,2},{1,3},{2,0},{3,1},{4,6},{5,7},{6,4},{7,5},{8,10},{9,11},{10,... | collective-permute-start | bytes 1572872 | tf_op jit(solution)/shard_map/ppermute | solution.py:62
  223.2 44.5 %collective-permute-start.10 = (bf16[128,2048]{1,0:T(8,128)(2,1)}, bf16[128,2048]{1,0:T(8,128)(2,1)S(1)}, u32[]{:S(2)}, u32[]{:S(2)}) collective-permute-start(bf16[128,2048]{1,0:T(8,128)(2,1)} %fusion.50), channel_id=1, source_target_pairs={{0,2},{1,3},{2,0},{3,1},{4,6},{5,7},{6,4},{7,5},{8,10},{9,11},{10,... | collective-permute-start | bytes 1572872 | tf_op jit(solution)/shard_map/ppermute | solution.py:62
  257.6 10.1 %collective-permute-start.22 = (bf16[128,2048]{1,0:T(8,128)(2,1)}, bf16[128,2048]{1,0:T(8,128)(2,1)}, u32[]{:S(2)}, u32[]{:S(2)}) collective-permute-start(bf16[128,2048]{1,0:T(8,128)(2,1)} %multiply_convert_fusion.1), channel_id=1, source_target_pairs={{0,8},{8,0},{16,24},{24,16},{1,9},{9,1},{17,25},{25,17},{2,10},{10... | collective-permute-start | bytes 1572872 | tf_op jit(solution)/shard_map/ppermute | solution.py:62
  273.2 11.7 %collective-permute-start.23 = (bf16[128,1024]{1,0:T(8,128)(2,1)S(1)}, bf16[128,1024]{1,0:T(8,128)(2,1)S(1)}, u32[]{:S(2)}, u32[]{:S(2)}) collective-permute-start(bf16[128,1024]{1,0:T(8,128)(2,1)S(1)} %slice_select_fusion.1), channel_id=1, source_target_pairs={{16,0},{24,8},{17,1},{25,9},{18,2},{26,10},{19,3},{27,11},{20,4},{... | collective-permute-start | bytes 786440 | tf_op jit(solution)/shard_map/ppermute | solution.py:105
  274.5 13.8 %collective-permute-start.13 = (bf16[128,2048]{1,0:T(8,128)(2,1)S(1)}, bf16[128,2048]{1,0:T(8,128)(2,1)S(1)}, u32[]{:S(2)}, u32[]{:S(2)}) collective-permute-start(bf16[128,2048]{1,0:T(8,128)(2,1)S(1)} %get-tuple-element.80), channel_id=1, source_target_pairs={{0,8},{8,0},{16,24},{24,16},{1,9},{9,1},{17,25},{25,17},{2,10},{10... | collective-permute-start | bytes 1572872 | tf_op jit(solution)/shard_map/ppermute | solution.py:62
  284.9 3.4 collective-permute-start.24
  287.1 16.7 %collective-permute-start.25 = (bf16[128,2048]{1,0:T(8,128)(2,1)S(1)}, bf16[128,2048]{1,0:T(8,128)(2,1)S(1)}, u32[]{:S(2)}, u32[]{:S(2)}) collective-permute-start(bf16[128,2048]{1,0:T(8,128)(2,1)S(1)} %get-tuple-element.79), channel_id=1, source_target_pairs={{0,8},{8,0},{16,24},{24,16},{1,9},{9,1},{17,25},{25,17},{2,10},{10... | collective-permute-start | bytes 1572872 | tf_op jit(solution)/shard_map/ppermute | solution.py:62
  291.3 10.6 %collective-permute-start.14 = (bf16[128,1024]{1,0:T(8,128)(2,1)S(1)}, bf16[128,1024]{1,0:T(8,128)(2,1)S(1)}, u32[]{:S(2)}, u32[]{:S(2)}) collective-permute-start(bf16[128,1024]{1,0:T(8,128)(2,1)S(1)} %slice_select_fusion.3), channel_id=1, source_target_pairs={{16,0},{24,8},{17,1},{25,9},{18,2},{26,10},{19,3},{27,11},{20,4},{... | collective-permute-start | bytes 786440 | tf_op jit(solution)/shard_map/ppermute | solution.py:105
  292.6 11.2 %collective-permute-start.17 = (bf16[128,2048]{1,0:T(8,128)(2,1)S(1)}, bf16[128,2048]{1,0:T(8,128)(2,1)S(1)}, u32[]{:S(2)}, u32[]{:S(2)}) collective-permute-start(bf16[128,2048]{1,0:T(8,128)(2,1)S(1)} %get-tuple-element.81), channel_id=1, source_target_pairs={{0,8},{8,0},{16,24},{24,16},{1,9},{9,1},{17,25},{25,17},{2,10},{10... | collective-permute-start | bytes 1572872 | tf_op jit(solution)/shard_map/ppermute | solution.py:62
  308.6 11.2 %collective-permute-start.18 = (bf16[128,1024]{1,0:T(8,128)(2,1)S(1)}, bf16[128,1024]{1,0:T(8,128)(2,1)S(1)}, u32[]{:S(2)}, u32[]{:S(2)}) collective-permute-start(bf16[128,1024]{1,0:T(8,128)(2,1)S(1)} %slice_select_fusion.2), channel_id=1, source_target_pairs={{16,0},{24,8},{17,1},{25,9},{18,2},{26,10},{19,3},{27,11},{20,4},{... | collective-permute-start | bytes 786440 | tf_op jit(solution)/shard_map/ppermute | solution.py:105
  310.1 14.7 %collective-permute-start.26 = (bf16[128,1024]{1,0:T(8,128)(2,1)S(1)}, bf16[128,1024]{1,0:T(8,128)(2,1)}, u32[]{:S(2)}, u32[]{:S(2)}) collective-permute-start(bf16[128,1024]{1,0:T(8,128)(2,1)S(1)} %slice_select_fusion), channel_id=1, source_target_pairs={{16,0},{24,8},{17,1},{25,9},{18,2},{26,10},{19,3},{27,11},{20,4},{... | collective-permute-start | bytes 786440 | tf_op jit(solution)/shard_map/ppermute | solution.py:105
  319.8 14.7 %collective-permute-start.19 = (bf16[128,1024]{1,0:T(8,128)(2,1)S(1)}, bf16[128,1024]{1,0:T(8,128)(2,1)}, u32[]{:S(2)}, u32[]{:S(2)}) collective-permute-start(bf16[128,1024]{1,0:T(8,128)(2,1)S(1)} %collective-permute-done.18), channel_id=1, source_target_pairs={{0,8},{8,0},{1,9},{9,1},{2,10},{10,2},{3,11},{11,3},{4,12},{12,4},... | collective-permute-start | bytes 786440 | tf_op jit(solution)/shard_map/ppermute | solution.py:106
  324.7 9.8 %collective-permute-start.27 = (bf16[128,1024]{1,0:T(8,128)(2,1)}, bf16[128,1024]{1,0:T(8,128)(2,1)}, u32[]{:S(2)}, u32[]{:S(2)}) collective-permute-start(bf16[128,1024]{1,0:T(8,128)(2,1)} %collective-permute-done.26), channel_id=1, source_target_pairs={{0,8},{8,0},{1,9},{9,1},{2,10},{10,2},{3,11},{11,3},{4,12},{12,4},... | collective-permute-start | bytes 786440 | tf_op jit(solution)/shard_map/ppermute | solution.py:106
  327.3 6.6 %collective-permute-start.28 = (f32[128]{0:T(128)}, f32[128]{0:T(128)}, u32[]{:S(2)}, u32[]{:S(2)}) collective-permute-start(f32[128]{0:T(128)} %fusion.67), channel_id=1, source_target_pairs={{0,8},{8,0},{16,24},{24,16},{1,9},{9,1},{17,25},{25,17},{2,10},{10... | collective-permute-start | bytes 1544 | tf_op jit(solution)/shard_map/ppermute | solution.py:62
  331.3 6.7 %collective-permute-start.30 = (f32[128]{0:T(128)}, f32[128]{0:T(128)S(1)}, u32[]{:S(2)}, u32[]{:S(2)}) collective-permute-start(f32[128]{0:T(128)} %fusion.67), channel_id=1, source_target_pairs={{16,8},{24,0},{17,9},{25,1},{18,10},{26,2},{19,11},{27,3},{20,12},... | collective-permute-start | bytes 1544 | tf_op jit(solution)/shard_map/ppermute | solution.py:268
  332.6 5.5 %collective-permute-start.29 = (f32[128]{0:T(128)}, f32[128]{0:T(128)S(1)}, u32[]{:S(2)}, u32[]{:S(2)}) collective-permute-start(f32[128]{0:T(128)} %fusion.67), channel_id=1, source_target_pairs={{16,0},{24,8},{17,1},{25,9},{18,2},{26,10},{19,3},{27,11},{20,4},{... | collective-permute-start | bytes 1544 | tf_op jit(solution)/shard_map/ppermute | solution.py:267
  (69 other events, 722.5 us)
where the time goes:
time: 349 us; the launch traced here: 344 us
  waiting for transfers between devices  166 us (48%)
  local copies, waits for them, and re-layouts  55.7 us (16%)
  other arithmetic  46.2 us (13%)
  starting transfers between devices  45.8 us (13%)
  matrix products  28.3 us (8%)
    ppermute x20, waiting for transfers between devices, swap(): return lax.ppermute(value, axis, [(i, i ^ bit) for i in range(count)])  134 us
    ppermute x4, waiting for transfers between devices, suffix_sum(): got = lax.ppermute(part, 'section', [(2, 0), (3, 1)])  29.4 us
    ppermute x20, starting transfers between devices, swap(): return lax.ppermute(value, axis, [(i, i ^ bit) for i in range(count)])  18.7 us
    unnamed x140, local copies, waits for them, and re-layouts  17.6 us
    sub x2, matrix products, attend_group(): exponent = jnp.exp(scores - row_max)  9.65 us
    slice x1, local copies, waits for them, and re-layouts, on_device(): owns = [weight[chunk * step:(chunk + 1) * step] for chunk in range(CHUNKS)]  9.3 us
    ppermute x4, starting transfers between devices, suffix_sum(): other = lax.ppermute(got, 'section', [(0, 1), (1, 0)])  7.89 us
    dot_general x8, matrix products, times_weight(): lax.dot_general(rows, weight, (((last - 1, last), (1, 2)), ((), ())), pre...  7.77 us
  transfers between devices with their start and end apart: 33, of which 15 were waited for; matrix products, arithmetic and copies ran while one was open for 31% of the time, Pallas kernels for 0%

commit v1 on v0

--- a/solution.py
+++ b/solution.py
@@ -10,7 +10,7 @@
 MASKED_SCORE = -1e30
 EPSILON = 1e-05
 CHUNKS = 4
-AHEAD = 2
+LOADS = 2
 
 
 def visible_keys(seg_row, prompt_row, table, page_ids):
@@ -68,14 +68,14 @@
     return lax.all_gather(value, "sample", axis=axis, tiled=True)
 
 
-def sample_reduce(value):
-    count = lax.axis_size("sample")
-    rows = value.shape[0] // count
-    if count == 2:
-        theirs = swap(value[rows:].astype(jnp.bfloat16), "sample", 1)
-        return value[:rows] + theirs.astype(jnp.float32)
+def sample_sum(value):
     low = value.astype(jnp.bfloat16)
-    return lax.psum_scatter(low, "sample", scatter_dimension=0, tiled=True).astype(jnp.float32)
+    if lax.axis_size("sample") == 2:
+        half = value.shape[0] // 2
+        theirs = swap(low, "sample", 1)
+        theirs = jnp.concatenate([theirs[half:], theirs[:half]], axis=0)
+        return (value + theirs.astype(jnp.float32)).astype(jnp.bfloat16)
+    return lax.psum(low, "sample")
 
 
 def times_weight(rows, weight):
@@ -89,25 +89,11 @@
     return lax.optimization_barrier(values)
 
 
-def suffix_sum(term):
+def suffix_all(term):
     count = lax.axis_size("section")
-    place = lax.axis_index("section")
-    low = term.astype(jnp.bfloat16)
-    if count != 4:
-        gathered = lax.all_gather(low, "section").astype(jnp.float32)
-        above = (jnp.arange(count) > place)[:, None, None]
-        return term + jnp.sum(jnp.where(above, gathered, 0.0), axis=0)
-    odd = place % 2 == 1
-    half = term.shape[1] // 2
-    peer = swap(low, "section", 1).astype(jnp.float32)
-    pair = (term + peer).astype(jnp.bfloat16)
-    part = jnp.where(odd, pair[:, half:], pair[:, :half])
-    got = lax.ppermute(part, "section", [(2, 0), (3, 1)])
-    other = lax.ppermute(got, "section", [(0, 1), (1, 0)])
-    upper = jnp.where(
-        odd, jnp.concatenate([other, got], axis=1), jnp.concatenate([got, other], axis=1)
-    )
-    return term + jnp.where(odd, 0.0, peer) + upper.astype(jnp.float32)
+    gathered = lax.all_gather(term.astype(jnp.bfloat16), "section").astype(jnp.float32)
+    above = (jnp.arange(count) > lax.axis_index("section"))[:, None, None]
+    return term + jnp.sum(jnp.where(above, gathered, 0.0), axis=0)
 
 
 def from_above(value, step):
@@ -148,12 +134,20 @@
 
     weight = kv_weight[0]
     width = weight.shape[0]
-    step = width // CHUNKS
-    piece = step // samples
-    partner_half = []
-    for chunk in range(AHEAD):
-        mine = lax.dynamic_slice_in_dim(weight, chunk * step + sample * piece, piece, 0)
-        partner_half.append(swap(mine, "tensor", 1))
+    share = width // samples
+    piece = share // CHUNKS
+    load = share // LOADS
+    owns = [
+        lax.dynamic_slice_in_dim(weight, sample * share + part * load, load, 0)
+        for part in range(LOADS)
+    ]
+    partner_weight = [swap(own, "tensor", 1) for own in owns]
+    early = LOADS // 2
+
+    def chunk_of(parts, chunk):
+        held = CHUNKS // LOADS
+        first = chunk % held * piece
+        return parts[chunk // held][first : first + piece]
 
     states_low = prefix_states[0]
     if sections == 4:
@@ -169,19 +163,16 @@
     grad_rows = output_grad[0].reshape(tok_count, kv_local, group_size, HEAD_SIZE)
     own_keys = suffix_keys[0]
     own_values = suffix_values[0]
-    query_pieces, suffix_key_pieces, suffix_value_pieces, prefix_key_pieces, prefix_value_pieces = (
-        [],
-        [],
-        [],
-        [],
-        [],
-    )
+    high, low = tensor // 2, tensor % 2
+    own_rows = pooled_rows // samples // tensors
+    query_pieces, suffix_key_pieces, suffix_value_pieces = [], [], []
+    full_pieces, keep_pieces, partner_pieces = [], [], []
     for head_index in range(kv_local):
         low_col = head_index * HEAD_SIZE
         cols = slice(low_col, low_col + HEAD_SIZE)
         if head_index == 1:
-            key_pool, value_pool, partner_half, states_across = tied(
-                key_pool, value_pool, partner_half, states_across
+            key_pool, value_pool, partner_weight[:early], states_across = tied(
+                key_pool, value_pool, partner_weight[:early], states_across
             )
         key_rows = jnp.concatenate([key_pool[:, cols], own_keys[:, cols]], axis=0)
         value_rows = jnp.concatenate([value_pool[:, cols], own_values[:, cols]], axis=0)
@@ -189,17 +180,18 @@
             query_rows[:, head_index], grad_rows[:, head_index], key_rows, value_rows, visible
         )
         query_pieces.append(query_out)
-        prefix_key_pieces.append(key_result[:pooled_rows])
         suffix_key_pieces.append(key_result[pooled_rows:])
-        prefix_value_pieces.append(value_out[:pooled_rows])
         suffix_value_pieces.append(value_out[pooled_rows:])
+        pooled = jnp.concatenate([key_result[:pooled_rows], value_out[:pooled_rows]], axis=1)
+        full = sample_sum(pooled)
+        by_owner = full.reshape(samples, tensors // 2, 2, own_rows, 2, HEAD_SIZE)
+        full_pieces.append(by_owner)
+        keep_pieces.append(lax.dynamic_index_in_dim(by_owner, low, 2, False))
+        give = lax.dynamic_index_in_dim(by_owner, 1 - low, 2, False)
+        partner_pieces.append(swap(give, "tensor", 1))
     query_grad = jnp.stack(query_pieces, axis=1).reshape(tok_count, -1).astype(jnp.bfloat16)
     rollout_key_gradient = jnp.concatenate(suffix_key_pieces, axis=1).astype(jnp.bfloat16)
     suffix_value_grad = jnp.concatenate(suffix_value_pieces, axis=1).astype(jnp.bfloat16)
-    pooled = jnp.concatenate(prefix_key_pieces + prefix_value_pieces, axis=1)
-    reduced = sample_reduce(pooled).astype(jnp.bfloat16)
-
-    partner_weight = [sample_gather(half, 0) for half in partner_half]
     if sections == 4:
         states_above = [
             swap(states_low, "section", 1),
@@ -208,71 +200,126 @@
         ]
     else:
         states_above = states_across
-    reduced, partner_weight, states_above = tied(reduced, partner_weight, states_above)
-
-    own_rows = reduced.shape[0] // tensors
-    high, low = tensor // 2, tensor % 2
-    by_owner = reduced.reshape(tensors // 2, 2, own_rows, 2, head_width)
-    keep = lax.dynamic_index_in_dim(by_owner, low, 1, False)
-    give = lax.dynamic_index_in_dim(by_owner, 1 - low, 1, False)
-    partner = swap(give, "tensor", 1)
-    here = lambda rows: lax.dynamic_index_in_dim(rows, high, 0, False)
-    there = lambda rows: lax.dynamic_index_in_dim(rows, 1 - high, 0, False)
+    partner_pieces, partner_weight, states_above = tied(
+        partner_pieces, partner_weight, states_above
+    )
+    keep = jnp.concatenate(keep_pieces, axis=-1)
+    partner = jnp.concatenate(partner_pieces, axis=-1)
+    full = jnp.concatenate(full_pieces, axis=-1)
+    at_home = 0 if samples == 2 else sample
+    reduced = lax.dynamic_index_in_dim(full, at_home, 0, False).reshape(-1, 2, head_width)
+    here = lambda rows: lax.dynamic_index_in_dim(rows, high, 1, False)
+    there = lambda rows: lax.dynamic_index_in_dim(rows, 1 - high, 1, False)
 
     gain_wide = norm_gain[0].astype(jnp.float32)[None, :]
     states = states_low.astype(jnp.float32)
     inv_rms = lax.rsqrt(jnp.mean(states * states, axis=1, keepdims=True) + EPSILON)
 
-    def partner_product(rows, chunk):
-        pieces = times_weight(rows, partner_weight[chunk])
-        if samples != 2:
-            return pieces
-        turned = jnp.concatenate([pieces[..., piece:], pieces[..., :piece]], axis=-1)
-        return jnp.where(sample == 0, pieces, turned)
-
-    owns = [weight[chunk * step : (chunk + 1) * step] for chunk in range(CHUNKS)]
-    local, sent, theirs = {}, {}, {}
-    for chunk in range(AHEAD, CHUNKS):
-        theirs[chunk] = swap(
-            times_weight(give, owns[chunk]).astype(jnp.bfloat16), "tensor", 1
+    keep_here, keep_there = here(keep), there(keep)
+    partner_here, partner_there = here(partner), there(partner)
+    local, sent = [], []
+    for chunk in range(CHUNKS):
+        total = times_weight(keep_there, chunk_of(owns, chunk)) + times_weight(
+            partner_there, chunk_of(partner_weight, chunk)
         )
-    for chunk in range(AHEAD):
-        total = times_weight(keep, owns[chunk]) + partner_product(partner, chunk)
-        sent[chunk] = swap(there(total).astype(jnp.bfloat16), "tensor", 2)
-        local[chunk] = here(total)
-    for chunk in range(AHEAD, CHUNKS):
-        total = times_weight(keep, owns[chunk]) + theirs[chunk].astype(jnp.float32)
-        sent[chunk] = swap(there(total).astype(jnp.bfloat16), "tensor", 2)
-        local[chunk] = here(total)
+        sent.append(swap(total.astype(jnp.bfloat16), "tensor", 2))
+    for chunk in range(CHUNKS):
+        local.append(
+            times_weight(keep_here, chunk_of(owns, chunk))
+            + times_weight(partner_here, chunk_of(partner_weight, chunk))
+        )
 
     home = lax.all_to_all(
-        reduced.reshape(-1, 2, head_width), "tensor", split_axis=0, concat_axis=2, tiled=True
+        reduced, "tensor", split_axis=0, concat_axis=2, tiled=True
     ).astype(jnp.float32)
     last = CHUNKS - 1
     sent[last], home, query_grad, rollout_key_gradient, suffix_value_grad = tied(
         sent[last], home, query_grad, rollout_key_gradient, suffix_value_grad
     )
 
-    sums, along = [], 0.0
-    for chunk in range(CHUNKS):
-        cols = slice(chunk * step, (chunk + 1) * step)
-        normed = local[chunk] + sent[chunk].astype(jnp.float32)
-        gained = gain_wide[:, cols] * normed
-        along = along + jnp.sum(states[:, cols] * gained, axis=1)
-        sums.append(suffix_sum(inv_rms * gained))
+    odd = lax.axis_index("section") % 2 == 1
+
+    def of_chunk(rows, chunk):
+        parts = rows.reshape(rows.shape[0], samples, CHUNKS, piece)
+        return parts[:, :, chunk].reshape(rows.shape[0], samples * piece)
+
+    def to_samples(chunk, arrived):
+        normed = local[chunk] + arrived.astype(jnp.float32)
+        if samples == 2:
+            return normed[0], swap(normed[1].astype(jnp.bfloat16), "sample", 1)
+        return None, lax.all_to_all(normed.astype(jnp.bfloat16), "sample", 0, 0, tiled=True)
+
+    def whole_chunk(mine, arrived):
+        arrived = arrived.astype(jnp.float32)
+        if samples == 2:
+            return jnp.where(
+                sample == 0,
+                jnp.concatenate([mine, arrived], axis=1),
+                jnp.concatenate([arrived, mine], axis=1),
+            )
+        return jnp.concatenate([arrived[i] for i in range(samples)], axis=1)
+
+    sums, along = [None] * CHUNKS, 0.0
+    mine, at_sample, terms, at_core = {}, {}, {}, {}
+    peers, at_across, at_back, got = {}, {}, {}, {}
+    for tick in range(CHUNKS + 4):
+        if tick < CHUNKS:
+            waiting = [
+                (held, tick - 1 - place)
+                for place, held in enumerate((at_sample, at_core, at_across, at_back))
+                if tick - 1 - place in held
+            ]
+            sent[tick], ready = tied(sent[tick], [held[key] for held, key in waiting])
+            for (held, key), value in zip(waiting, ready):
+                held[key] = value
+        chunk = tick - 4
+        if chunk >= 0 and sections == 4:
+            upper = jnp.where(
+                odd,
+                jnp.concatenate([at_back[chunk], got[chunk]], axis=1),
+                jnp.concatenate([got[chunk], at_back[chunk]], axis=1),
+            )
+            below = terms[chunk] + jnp.where(odd, 0.0, peers[chunk])
+            sums[chunk] = below + upper.astype(jnp.float32)
+        chunk = tick - 3
+        if 0 <= chunk < CHUNKS and sections == 4:
+            got[chunk] = at_across[chunk]
+            at_back[chunk] = lax.ppermute(got[chunk], "section", [(0, 1), (1, 0)])
+        chunk = tick - 2
+        if 0 <= chunk < CHUNKS and sections == 4:
+            peers[chunk] = at_core[chunk].astype(jnp.float32)
+            pair = (terms[chunk] + peers[chunk]).astype(jnp.bfloat16)
+            half = pair.shape[1] // 2
+            part = jnp.where(odd, pair[:, half:], pair[:, :half])
+            at_across[chunk] = lax.ppermute(part, "section", [(2, 0), (3, 1)])
+        chunk = tick - 1
+        if 0 <= chunk < CHUNKS:
+            gained = of_chunk(gain_wide, chunk) * whole_chunk(mine[chunk], at_sample[chunk])
+            along = along + jnp.sum(of_chunk(states, chunk) * gained, axis=1)
+            terms[chunk] = inv_rms * gained
+            if sections == 4:
+                at_core[chunk] = swap(terms[chunk].astype(jnp.bfloat16), "section", 1)
+            else:
+                sums[chunk] = suffix_all(terms[chunk])
+        if tick < CHUNKS:
+            mine[tick], at_sample[tick] = to_samples(tick, sent[tick])
     slope = inv_rms[:, 0] ** 3 * (along / width)
     state_part = states * slope[:, None]
     if sections == 4:
         peer = swap(slope, "section", 1)
         across = lax.ppermute(slope, "section", [(2, 0), (3, 1)])
         across_peer = lax.ppermute(slope, "section", [(2, 1), (3, 0)])
-        odd = lax.axis_index("section") % 2 == 1
         slopes_above = [jnp.where(odd, 0.0, peer), across, across_peer]
     else:
         slopes_above = [from_above(slope, hop) for hop in range(1, sections)]
     for above, slope_above in zip(states_above, slopes_above):
         state_part = state_part + above.astype(jnp.float32) * slope_above[:, None]
-    prefix_state_gradient = jnp.concatenate(sums, axis=1) - state_part
+    ordered = [
+        sums[chunk][:, part * piece : (part + 1) * piece]
+        for part in range(samples)
+        for chunk in range(CHUNKS)
+    ]
+    prefix_state_gradient = jnp.concatenate(ordered, axis=1) - state_part
 
     return (
         query_grad[None],

time: 349 us -> 366 us (1.049)
  waiting for transfers between devices: 166 us -> 115 us
  local copies, waits for them, and re-layouts: 55.7 us -> 84.1 us
  matrix products: 28.3 us -> 49.6 us
  other arithmetic: 46.2 us -> 59.5 us
  starting transfers between devices: 45.8 us -> 50 us
    ppermute x20 -> x22, waiting for transfers between devices: 134 us -> 101 us  [swap(): return lax.ppermute(value, axis, [(i, i ^ bit) for i in range(count)])]
    unnamed x140 -> x167, local copies, waits for them, and re-layouts: 17.6 us -> 38.3 us
    dot_general x8 -> x16, matrix products: 7.77 us -> 27.9 us  [times_weight(): lax.dot_general(rows, weight, (((last - 1, last), (1, 2)), ((), ())), pre...]
    ppermute x8, waiting for transfers between devices: 31.6 us -> 13.9 us  [the longest x4 13.5 us: on_device(): at_across[chunk] = lax.ppermute(part, 'section', [(2, 0), (3, 1)])]
    convert_element_type x5 -> x12, other arithmetic: 8.97 us -> 16.9 us  [the longest x3 5.7 us: on_device(): pair = (terms[chunk] + peers[chunk]).astype(jnp.bfloat16)]
    concatenate x0 -> x6, local copies, waits for them, and re-layouts: none -> 6.74 us  [the longest x4 5.68 us: whole_chunk(): jnp.concatenate([mine, arrived], axis=1)]
    slice x11 -> x8, local copies, waits for them, and re-layouts: 11.6 us -> 5.01 us  [the longest x2 2.71 us: of_chunk(): return parts[:, :, chunk].reshape(rows.shape[0], samples * piece)]
    dynamic_slice x4 -> x3, local copies, waits for them, and re-layouts: 7.52 us -> 11.5 us  [the longest x1 4.68 us: on_device(): lax.dynamic_slice_in_dim(weight, sample * share + part * load, load, 0)]
  transfers between devices with their start and end apart: 33 -> 35, of which waited for: 15 -> 13; matrix products, arithmetic and copies ran while one was open for 31% -> 42% of each run, Pallas kernels for 0% -> 0%
where the time goes in v1:
time: 366 us; the launch traced here: 360 us
  waiting for transfers between devices  115 us (31%)
  local copies, waits for them, and re-layouts  84.1 us (23%)
  other arithmetic  59.5 us (16%)
  starting transfers between devices  50 us (14%)
  matrix products  49.6 us (14%)
    ppermute x22, waiting for transfers between devices, swap(): return lax.ppermute(value, axis, [(i, i ^ bit) for i in range(count)])  101 us
    unnamed x167, local copies, waits for them, and re-layouts  38.3 us
    dot_general x16, matrix products, times_weight(): lax.dot_general(rows, weight, (((last - 1, last), (1, 2)), ((), ())), pre...  27.9 us
    ppermute x22, starting transfers between devices, swap(): return lax.ppermute(value, axis, [(i, i ^ bit) for i in range(count)])  21.8 us
    ppermute x4, waiting for transfers between devices, on_device(): at_across[chunk] = lax.ppermute(part, 'section', [(2, 0), (3, 1)])  13.5 us
    sub x2, matrix products, attend_group(): exponent = jnp.exp(scores - row_max)  9.7 us
    ppermute x4, starting transfers between devices, on_device(): at_back[chunk] = lax.ppermute(got[chunk], 'section', [(0, 1), (1, 0)])  7.64 us
  transfers between devices with their start and end apart: 35, of which 13 were waited for; matrix products, arithmetic and copies ran while one was open for 42% of the time, Pallas kernels for 0%

profile of v1, /device:TPU:0, one launch (start us, length us, event | category | flops | bytes accessed | tf_op | source)
XLA Modules:
  0.0 360.0 jit_solution(3391863110514500505)
XLA Ops:
  4.6 5.9 %all-to-all-start = ((bf16[2,128,1024]{1,0,2:T(2,128)(2,1)}), bf16[2,128,1024]{1,0,2:T(2,128)(2,1)S(1)}, u32[]{:S(2)}, u32[]{:S(2)}) async-start(bf16[2,128,1024]{1,0,2:T(2,128)(2,1)} %copy.236), calls=%async_computation | async-start | bytes 1048576 | tf_op jit(solution)/shard_map/all_to_all | solution.py:126
  10.5 4.7 %constant_dynamic-slice_fusion.2 = (bf16[1,2048,2,256]{3,2,1,0:T(2,128)(2,1)S(1)}, bf16[1,2048,2,256]{3,2,1,0:T(2,128)(2,1)S(1)}) fusion(bf16[1,8192,2,256]{3,2,1,0:T(2,128)(2,1)} %param.18, s32[]{:T(128)S(6)} %select_n.195, s32[]{:T(128)S(6)} %select_n.191), kind=kLoop, calls=%fused_computation.266 | loop fusion | bytes 8388616 | tf_op jit(solution)/shard_map/dynamic_slice | solution.py:141
  35.1 10.2 %collective-permute-done = bf16[2,512,256]{2,1,0:T(8,128)(2,1)S(1)} collective-permute-done((bf16[2,512,256]{2,1,0:T(8,128)(2,1)}, bf16[2,512,256]{2,1,0:T(8,128)(2,1)S(1)}, u32[]{:S(2)}, u32[]{:S(2)}) %collective-permute-start) | collective-permute-done | bytes 524320 | tf_op jit(solution)/shard_map/ppermute | solution.py:62
  47.2 4.9 %exponential_reduce_fusion.1 = (f32[128,8]{0,1:T(8,128)S(1)}, f32[128,8,1152]{0,2,1:T(8,128)}) fusion(pred[128,1152]{0,1:T(8,128)(4,1)} %pad_add_fusion, bf16[128,2,8,128]{0,3,2,1:T(8,128)(2,1)} %bitcast.363, bf16[128,128]{1,0:T(8,128)(2,1)S(1)} %copy-done.60, bf16[1024,128]{1,0:T(8,128)(2,1)S(1)} %slice.307), kind=kOutput, calls=%fused_computation.21 | convolution fusion | flops 307299456 | bytes 5427200 | tf_op jit(solution)/shard_map/sub | solution.py:37
  52.1 3.1 fusion.20
  63.0 4.8 %collective-permute-done.2 = bf16[2048,2,256]{2,0,1:T(8,128)(2,1)} collective-permute-done((bf16[2048,2,256]{2,0,1:T(8,128)(2,1)}, bf16[2048,2,256]{2,0,1:T(8,128)(2,1)}, u32[]{:S(2)}, u32[]{:S(2)}) %collective-permute-start.2) | collective-permute-done | bytes 2097184 | tf_op jit(solution)/shard_map/ppermute | solution.py:62
  68.6 4.8 %exponential_reduce_fusion = (f32[128,8]{0,1:T(8,128)S(1)}, f32[128,8,1152]{0,2,1:T(8,128)}) fusion(pred[128,1152]{0,1:T(8,128)(4,1)} %pad_add_fusion, bf16[128,2,8,128]{0,3,2,1:T(8,128)(2,1)} %bitcast.364, bf16[128,128]{1,0:T(8,128)(2,1)S(1)} %copy-done.59, bf16[1024,128]{1,0:T(8,128)(2,1)S(1)} %slice.245), kind=kOutput, calls=%fused_computation.19 | convolution fusion | flops 307299456 | bytes 5427200 | tf_op jit(solution)/shard_map/sub | solution.py:37
  73.4 3.1 fusion.21
  91.9 5.1 %collective-permute-done.4 = bf16[1024,256]{0,1:T(8,128)(2,1)} collective-permute-done((bf16[1024,256]{0,1:T(8,128)(2,1)}, bf16[1024,256]{0,1:T(8,128)(2,1)}, u32[]{:S(2)}, u32[]{:S(2)}) %collective-permute-start.4) | collective-permute-done | bytes 524320 | tf_op jit(solution)/shard_map/ppermute | solution.py:62
  98.0 2.1 add_convert_fusion
  103.1 3.5 copy.264
  106.5 5.3 %all-to-all-start.1 = ((bf16[512,2,256]{2,1,0:T(2,128)(2,1)}), bf16[512,2,256]{2,1,0:T(2,128)(2,1)}, u32[]{:S(2)}, u32[]{:S(2)}) async-start(bf16[512,2,256]{2,1,0:T(2,128)(2,1)} %bitcast.360), calls=%async_computation.1 | async-start | bytes 1048576 | tf_op jit(solution)/shard_map/all_to_all | solution.py:232
  111.8 2.9 fusion.38
  114.7 3.3 constant_dynamic-slice_fusion.3
  130.5 4.4 %collective-permute-done.6 = bf16[2,2,128,2,128]{4,2,3,1,0:T(8,128)(2,1)} collective-permute-done((bf16[2,2,128,2,128]{4,2,3,1,0:T(8,128)(2,1)}, bf16[2,2,128,2,128]{4,2,3,1,0:T(8,128)(2,1)}, u32[]{:S(2)}, u32[]{:S(2)}) %collective-permute-start.6) | collective-permute-done | bytes 262176 | tf_op jit(solution)/shard_map/ppermute | solution.py:62
  147.2 2.5 fusion.33
  164.3 67.9 %collective-permute-done.11 = bf16[2,128,1024]{2,1,0:T(8,128)(2,1)S(1)} collective-permute-done((bf16[2,128,1024]{2,1,0:T(8,128)(2,1)S(1)}, bf16[2,128,1024]{2,1,0:T(8,128)(2,1)S(1)}, u32[]{:S(2)}, u32[]{:S(2)}) %collective-permute-start.11) | collective-permute-done | bytes 524320 | tf_op jit(solution)/shard_map/ppermute | solution.py:62
  236.6 5.6 %collective-permute-done.12 = bf16[2,128,1024]{2,1,0:T(8,128)(2,1)S(1)} collective-permute-done((bf16[2,128,1024]{2,1,0:T(8,128)(2,1)S(1)}, bf16[2,128,1024]{2,1,0:T(8,128)(2,1)S(1)}, u32[]{:S(2)}, u32[]{:S(2)}) %collective-permute-start.12) | collective-permute-done | bytes 524320 | tf_op jit(solution)/shard_map/ppermute | solution.py:62
  258.7 2.6 copy.266
  263.2 5.5 %collective-permute-done.19 = bf16[128,1024]{1,0:T(8,128)(2,1)} collective-permute-done((bf16[128,1024]{1,0:T(8,128)(2,1)}, bf16[128,1024]{1,0:T(8,128)(2,1)}, u32[]{:S(2)}, u32[]{:S(2)}) %collective-permute-start.19) | collective-permute-done | bytes 262176 | tf_op jit(solution)/shard_map/ppermute | solution.py:294
  280.7 2.4 copy.276
  283.1 3.7 %collective-permute-done.24 = bf16[128,1024]{1,0:T(8,128)(2,1)S(1)} collective-permute-done((bf16[128,1024]{1,0:T(8,128)(2,1)}, bf16[128,1024]{1,0:T(8,128)(2,1)S(1)}, u32[]{:S(2)}, u32[]{:S(2)}) %collective-permute-start.24) | collective-permute-done | bytes 262176 | tf_op jit(solution)/shard_map/ppermute | solution.py:294
  292.6 3.4 fusion.153
  301.1 2.6 copy.340
  303.7 2.5 copy.339
  306.2 2.5 copy.337
  308.7 2.6 copy.338
  312.7 4.0 %fusion.51 = (bf16[128,2048]{1,0:T(8,128)(2,1)S(1)}, f32[128,2048]{1,0:T(8,128)}) fusion(bf16[128,2048]{1,0:T(8,128)(2,1)} %collective-permute-done.27, f32[128,1024]{1,0:T(8,128)} %copy-done.7, f32[128,1024]{1,0:T(8,128)} %copy-done.9, pred[]{:T(512)S(6)} %eq.85, f32[2048]{0:T(1024)S(1)} %bitcast.378, f32[128]{0:T(128)} %add_rsqrt_fusion, ...), kind=kLoop, calls=%fused_computation.97 | loop fusion | flops 7077888 | bytes 5259778 | tf_op jit(solution)/shard_map/convert_element_type | solution.py:291
  322.8 2.2 fusion.62
  325.0 3.3 collective-permute-done.28
  332.7 3.1 fusion.50
  352.7 7.1 %fusion.13 = f32[1,128,8192]{2,1,0:T(8,128)} fusion(f32[128,8192]{1,0:T(8,128)S(1)} %slice_dynamic-update-slice_fusion, bf16[128,8192]{1,0:T(8,128)(2,1)} %collective-permute-done.9, bf16[128,8192]{1,0:T(8,128)(2,1)} %collective-permute-done.3, bf16[128,8192]{1,0:T(8,128)(2,1)} %collective-permute-done.8, f32[128]{0:T(128)S(1)} %collective-permute-done.32, ...), kind=kLoop, calls=%fused_computation.27 | loop fusion | flops 12582912 | bytes 16779264 | tf_op jit(solution)/shard_map/broadcast_in_dim | solution.py:330
  (327 shorter events, 166.2 us)
Async XLA Ops:
  0.6 67.2 %collective-permute-start.3 = (bf16[128,8192]{1,0:T(8,128)(2,1)}, bf16[128,8192]{1,0:T(8,128)(2,1)}, u32[]{:S(2)}, u32[]{:S(2)}) collective-permute-start(bf16[128,8192]{1,0:T(8,128)(2,1)} %bitcast.348), channel_id=1, source_target_pairs={{16,0},{24,8},{17,1},{25,9},{18,2},{26,10},{19,3},{27,11},{20,4},{... | collective-permute-start | bytes 6291464 | tf_op jit(solution)/shard_map/ppermute | solution.py:154
  1.9 127.7 %collective-permute-start.8 = (bf16[128,8192]{1,0:T(8,128)(2,1)}, bf16[128,8192]{1,0:T(8,128)(2,1)}, u32[]{:S(2)}, u32[]{:S(2)}) collective-permute-start(bf16[128,8192]{1,0:T(8,128)(2,1)} %bitcast.349), channel_id=1, source_target_pairs={{0,8},{8,0},{16,24},{24,16},{1,9},{9,1},{17,25},{25,17},{2,10},{10... | collective-permute-start | bytes 6291464 | tf_op jit(solution)/shard_map/ppermute | solution.py:62
  4.6 25.6 %all-to-all-start = ((bf16[2,128,1024]{1,0,2:T(2,128)(2,1)}), bf16[2,128,1024]{1,0,2:T(2,128)(2,1)S(1)}, u32[]{:S(2)}, u32[]{:S(2)}) async-start(bf16[2,128,1024]{1,0,2:T(2,128)(2,1)} %copy.236), calls=%async_computation | async-start | bytes 1048576 | tf_op jit(solution)/shard_map/all_to_all | solution.py:126
  16.8 51.0 %collective-permute-start.2 = (bf16[2048,2,256]{2,0,1:T(8,128)(2,1)}, bf16[2048,2,256]{2,0,1:T(8,128)(2,1)}, u32[]{:S(2)}, u32[]{:S(2)}) collective-permute-start(bf16[2048,2,256]{2,0,1:T(8,128)(2,1)} %bitcast.317.clone.2), channel_id=1, source_target_pairs={{0,1},{1,0},{2,3},{3,2},{4,5},{5,4},{6,7},{7,6},{8,9},{9,8},{10,11... | collective-permute-start | bytes 6291464 | tf_op jit(solution)/shard_map/ppermute | solution.py:62
  20.5 109.2 %collective-permute-start.7 = (bf16[2048,2,256]{2,0,1:T(8,128)(2,1)}, bf16[2048,2,256]{2,0,1:T(8,128)(2,1)}, u32[]{:S(2)}, u32[]{:S(2)}) collective-permute-start(bf16[2048,2,256]{2,0,1:T(8,128)(2,1)} %bitcast.316.clone.2), channel_id=1, source_target_pairs={{0,1},{1,0},{2,3},{3,2},{4,5},{5,4},{6,7},{7,6},{8,9},{9,8},{10,11... | collective-permute-start | bytes 6291464 | tf_op jit(solution)/shard_map/ppermute | solution.py:62
  31.5 13.8 %collective-permute-start = (bf16[2,512,256]{2,1,0:T(8,128)(2,1)}, bf16[2,512,256]{2,1,0:T(8,128)(2,1)S(1)}, u32[]{:S(2)}, u32[]{:S(2)}) collective-permute-start(bf16[2,512,256]{2,1,0:T(8,128)(2,1)} %bitcast.361), channel_id=1, source_target_pairs={{0,4},{4,0},{1,5},{5,1},{2,6},{6,2},{3,7},{7,3},{8,12},{12,8},{9,1... | collective-permute-start | bytes 1572872 | tf_op jit(solution)/shard_map/ppermute | solution.py:62
  61.5 24.0 %collective-permute-start.1 = (bf16[1024,256]{0,1:T(8,128)(2,1)}, bf16[1024,256]{0,1:T(8,128)(2,1)}, u32[]{:S(2)}, u32[]{:S(2)}) collective-permute-start(bf16[1024,256]{0,1:T(8,128)(2,1)} %fusion.89), channel_id=1, source_target_pairs={{0,4},{4,0},{1,5},{5,1},{2,6},{6,2},{3,7},{7,3},{8,12},{12,8},{9,1... | collective-permute-start | bytes 1572872 | tf_op jit(solution)/shard_map/ppermute | solution.py:62
  79.5 55.5 %collective-permute-start.9 = (bf16[128,8192]{1,0:T(8,128)(2,1)}, bf16[128,8192]{1,0:T(8,128)(2,1)}, u32[]{:S(2)}, u32[]{:S(2)}) collective-permute-start(bf16[128,8192]{1,0:T(8,128)(2,1)} %collective-permute-done.3), channel_id=1, source_target_pairs={{0,8},{8,0},{16,24},{24,16},{1,9},{9,1},{17,25},{25,17},{2,10},{10... | collective-permute-start | bytes 6291464 | tf_op jit(solution)/shard_map/ppermute | solution.py:62
  82.3 14.6 %collective-permute-start.4 = (bf16[1024,256]{0,1:T(8,128)(2,1)}, bf16[1024,256]{0,1:T(8,128)(2,1)}, u32[]{:S(2)}, u32[]{:S(2)}) collective-permute-start(bf16[1024,256]{0,1:T(8,128)(2,1)} %fusion.88), channel_id=1, source_target_pairs={{0,4},{4,0},{1,5},{5,1},{2,6},{6,2},{3,7},{7,3},{8,12},{12,8},{9,1... | collective-permute-start | bytes 1572872 | tf_op jit(solution)/shard_map/ppermute | solution.py:62
  106.5 22.0 %all-to-all-start.1 = ((bf16[512,2,256]{2,1,0:T(2,128)(2,1)}), bf16[512,2,256]{2,1,0:T(2,128)(2,1)}, u32[]{:S(2)}, u32[]{:S(2)}) async-start(bf16[512,2,256]{2,1,0:T(2,128)(2,1)} %bitcast.360), calls=%async_computation.1 | async-start | bytes 1048576 | tf_op jit(solution)/shard_map/all_to_all | solution.py:232
  119.3 11.2 %collective-permute-start.5 = (bf16[2,2,128,2,128]{4,2,3,1,0:T(8,128)(2,1)S(1)}, bf16[2,2,128,2,128]{4,2,3,1,0:T(8,128)(2,1)}, u32[]{:S(2)}, u32[]{:S(2)}) collective-permute-start(bf16[2,2,128,2,128]{4,2,3,1,0:T(8,128)(2,1)S(1)} %bitcast.371), channel_id=1, source_target_pairs={{0,1},{1,0},{2,3},{3,2},{4,5},{5,4},{6,7},{7,6},{8,9},{9,8},{10,11... | collective-permute-start | bytes 786440 | tf_op jit(solution)/shard_map/ppermute | solution.py:62
  123.3 11.7 %collective-permute-start.6 = (bf16[2,2,128,2,128]{4,2,3,1,0:T(8,128)(2,1)}, bf16[2,2,128,2,128]{4,2,3,1,0:T(8,128)(2,1)}, u32[]{:S(2)}, u32[]{:S(2)}) collective-permute-start(bf16[2,2,128,2,128]{4,2,3,1,0:T(8,128)(2,1)} %bitcast.41), channel_id=1, source_target_pairs={{0,1},{1,0},{2,3},{3,2},{4,5},{5,4},{6,7},{7,6},{8,9},{9,8},{10,11... | collective-permute-start | bytes 786440 | tf_op jit(solution)/shard_map/ppermute | solution.py:62
  149.7 111.6 %collective-permute-start.10 = (bf16[2,128,1024]{2,1,0:T(8,128)(2,1)}, bf16[2,128,1024]{2,1,0:T(8,128)(2,1)}, u32[]{:S(2)}, u32[]{:S(2)}) collective-permute-start(bf16[2,128,1024]{2,1,0:T(8,128)(2,1)} %fusion.33), channel_id=1, source_target_pairs={{0,2},{1,3},{2,0},{3,1},{4,6},{5,7},{6,4},{7,5},{8,10},{9,11},{10,... | collective-permute-start | bytes 1572872 | tf_op jit(solution)/shard_map/ppermute | solution.py:62
  152.8 94.9 %collective-permute-start.14 = (bf16[2,128,1024]{2,1,0:T(8,128)(2,1)S(1)}, bf16[2,128,1024]{2,1,0:T(8,128)(2,1)S(1)}, u32[]{:S(2)}, u32[]{:S(2)}) collective-permute-start(bf16[2,128,1024]{2,1,0:T(8,128)(2,1)S(1)} %fusion.30), channel_id=1, source_target_pairs={{0,2},{1,3},{2,0},{3,1},{4,6},{5,7},{6,4},{7,5},{8,10},{9,11},{10,... | collective-permute-start | bytes 1572872 | tf_op jit(solution)/shard_map/ppermute | solution.py:62
  156.1 76.1 %collective-permute-start.11 = (bf16[2,128,1024]{2,1,0:T(8,128)(2,1)S(1)}, bf16[2,128,1024]{2,1,0:T(8,128)(2,1)S(1)}, u32[]{:S(2)}, u32[]{:S(2)}) collective-permute-start(bf16[2,128,1024]{2,1,0:T(8,128)(2,1)S(1)} %fusion.32), channel_id=1, source_target_pairs={{0,2},{1,3},{2,0},{3,1},{4,6},{5,7},{6,4},{7,5},{8,10},{9,11},{10,... | collective-permute-start | bytes 1572872 | tf_op jit(solution)/shard_map/ppermute | solution.py:62
  159.3 82.9 %collective-permute-start.12 = (bf16[2,128,1024]{2,1,0:T(8,128)(2,1)S(1)}, bf16[2,128,1024]{2,1,0:T(8,128)(2,1)S(1)}, u32[]{:S(2)}, u32[]{:S(2)}) collective-permute-start(bf16[2,128,1024]{2,1,0:T(8,128)(2,1)S(1)} %fusion.31), channel_id=1, source_target_pairs={{0,2},{1,3},{2,0},{3,1},{4,6},{5,7},{6,4},{7,5},{8,10},{9,11},{10,... | collective-permute-start | bytes 1572872 | tf_op jit(solution)/shard_map/ppermute | solution.py:62
  232.4 9.8 %collective-permute-start.13 = (bf16[128,1024]{1,0:T(8,128)(2,1)S(1)}, bf16[128,1024]{1,0:T(8,128)(2,1)S(1)}, u32[]{:S(2)}, u32[]{:S(2)}) collective-permute-start(bf16[128,1024]{1,0:T(8,128)(2,1)S(1)} %fusion.93), channel_id=1, source_target_pairs={{0,4},{4,0},{1,5},{5,1},{2,6},{6,2},{3,7},{7,3},{8,12},{12,8},{9,1... | collective-permute-start | bytes 786440 | tf_op jit(solution)/shard_map/ppermute | solution.py:62
  242.4 7.2 %collective-permute-start.15 = (bf16[128,1024]{1,0:T(8,128)(2,1)S(1)}, bf16[128,1024]{1,0:T(8,128)(2,1)S(1)}, u32[]{:S(2)}, u32[]{:S(2)}) collective-permute-start(bf16[128,1024]{1,0:T(8,128)(2,1)S(1)} %fusion.94), channel_id=1, source_target_pairs={{0,4},{4,0},{1,5},{5,1},{2,6},{6,2},{3,7},{7,3},{8,12},{12,8},{9,1... | collective-permute-start | bytes 786440 | tf_op jit(solution)/shard_map/ppermute | solution.py:62
  245.1 4.5 %collective-permute-start.16 = (bf16[128,2048]{1,0:T(8,128)(2,1)S(1)}, bf16[128,2048]{1,0:T(8,128)(2,1)S(1)}, u32[]{:S(2)}, u32[]{:S(2)}) collective-permute-start(bf16[128,2048]{1,0:T(8,128)(2,1)S(1)} %fusion.156), channel_id=1, source_target_pairs={{0,8},{8,0},{16,24},{24,16},{1,9},{9,1},{17,25},{25,17},{2,10},{10... | collective-permute-start | bytes 1572872 | tf_op jit(solution)/shard_map/ppermute | solution.py:62
  250.8 12.4 %collective-permute-start.17 = (bf16[128,1024]{1,0:T(8,128)(2,1)}, bf16[128,1024]{1,0:T(8,128)(2,1)}, u32[]{:S(2)}, u32[]{:S(2)}) collective-permute-start(bf16[128,1024]{1,0:T(8,128)(2,1)} %fusion.95), channel_id=1, source_target_pairs={{0,4},{4,0},{1,5},{5,1},{2,6},{6,2},{3,7},{7,3},{8,12},{12,8},{9,1... | collective-permute-start | bytes 786440 | tf_op jit(solution)/shard_map/ppermute | solution.py:62
  255.4 13.3 %collective-permute-start.18 = (bf16[128,2048]{1,0:T(8,128)(2,1)}, bf16[128,2048]{1,0:T(8,128)(2,1)}, u32[]{:S(2)}, u32[]{:S(2)}) collective-permute-start(bf16[128,2048]{1,0:T(8,128)(2,1)} %get-tuple-element.149), channel_id=1, source_target_pairs={{0,8},{8,0},{16,24},{24,16},{1,9},{9,1},{17,25},{25,17},{2,10},{10... | collective-permute-start | bytes 1572872 | tf_op jit(solution)/shard_map/ppermute | solution.py:62
  256.2 12.5 %collective-permute-start.19 = (bf16[128,1024]{1,0:T(8,128)(2,1)}, bf16[128,1024]{1,0:T(8,128)(2,1)}, u32[]{:S(2)}, u32[]{:S(2)}) collective-permute-start(bf16[128,1024]{1,0:T(8,128)(2,1)} %slice_select_fusion.3), channel_id=1, source_target_pairs={{16,0},{24,8},{17,1},{25,9},{18,2},{26,10},{19,3},{27,11},{20,4},{... | collective-permute-start | bytes 786440 | tf_op jit(solution)/shard_map/ppermute | solution.py:294
  276.0 10.8 %collective-permute-start.24 = (bf16[128,1024]{1,0:T(8,128)(2,1)}, bf16[128,1024]{1,0:T(8,128)(2,1)S(1)}, u32[]{:S(2)}, u32[]{:S(2)}) collective-permute-start(bf16[128,1024]{1,0:T(8,128)(2,1)} %slice_select_fusion.1), channel_id=1, source_target_pairs={{16,0},{24,8},{17,1},{25,9},{18,2},{26,10},{19,3},{27,11},{20,4},{... | collective-permute-start | bytes 786440 | tf_op jit(solution)/shard_map/ppermute | solution.py:294
  280.2 10.4 %collective-permute-start.26 = (bf16[128,1024]{1,0:T(8,128)(2,1)}, bf16[128,1024]{1,0:T(8,128)(2,1)}, u32[]{:S(2)}, u32[]{:S(2)}) collective-permute-start(bf16[128,1024]{1,0:T(8,128)(2,1)} %fusion.96), channel_id=1, source_target_pairs={{0,4},{4,0},{1,5},{5,1},{2,6},{6,2},{3,7},{7,3},{8,12},{12,8},{9,1... | collective-permute-start | bytes 786440 | tf_op jit(solution)/shard_map/ppermute | solution.py:62
  286.8 5.8 %collective-permute-start.25 = (bf16[128,1024]{1,0:T(8,128)(2,1)S(1)}, bf16[128,1024]{1,0:T(8,128)(2,1)S(1)}, u32[]{:S(2)}, u32[]{:S(2)}) collective-permute-start(bf16[128,1024]{1,0:T(8,128)(2,1)S(1)} %collective-permute-done.24), channel_id=1, source_target_pairs={{0,8},{8,0},{1,9},{9,1},{2,10},{10,2},{3,11},{11,3},{4,12},{12,4},... | collective-permute-start | bytes 786440 | tf_op jit(solution)/shard_map/ppermute | solution.py:287
  296.0 16.8 %collective-permute-start.27 = (bf16[128,2048]{1,0:T(8,128)(2,1)}, bf16[128,2048]{1,0:T(8,128)(2,1)}, u32[]{:S(2)}, u32[]{:S(2)}) collective-permute-start(bf16[128,2048]{1,0:T(8,128)(2,1)} %get-tuple-element.146), channel_id=1, source_target_pairs={{0,8},{8,0},{16,24},{24,16},{1,9},{9,1},{17,25},{25,17},{2,10},{10... | collective-permute-start | bytes 1572872 | tf_op jit(solution)/shard_map/ppermute | solution.py:62
  298.5 14.2 %collective-permute-start.20 = (bf16[128,1024]{1,0:T(8,128)(2,1)}, bf16[128,1024]{1,0:T(8,128)(2,1)S(1)}, u32[]{:S(2)}, u32[]{:S(2)}) collective-permute-start(bf16[128,1024]{1,0:T(8,128)(2,1)} %collective-permute-done.19), channel_id=1, source_target_pairs={{0,8},{8,0},{1,9},{9,1},{2,10},{10,2},{3,11},{11,3},{4,12},{12,4},... | collective-permute-start | bytes 786440 | tf_op jit(solution)/shard_map/ppermute | solution.py:287
  317.6 10.8 %collective-permute-start.28 = (bf16[128,1024]{1,0:T(8,128)(2,1)}, bf16[128,1024]{1,0:T(8,128)(2,1)S(1)}, u32[]{:S(2)}, u32[]{:S(2)}) collective-permute-start(bf16[128,1024]{1,0:T(8,128)(2,1)} %slice_select_fusion), channel_id=1, source_target_pairs={{16,0},{24,8},{17,1},{25,9},{18,2},{26,10},{19,3},{27,11},{20,4},{... | collective-permute-start | bytes 786440 | tf_op jit(solution)/shard_map/ppermute | solution.py:294
  336.6 10.8 %collective-permute-start.21 = (bf16[128,1024]{1,0:T(8,128)(2,1)}, bf16[128,1024]{1,0:T(8,128)(2,1)S(1)}, u32[]{:S(2)}, u32[]{:S(2)}) collective-permute-start(bf16[128,1024]{1,0:T(8,128)(2,1)} %slice_select_fusion.2), channel_id=1, source_target_pairs={{16,0},{24,8},{17,1},{25,9},{18,2},{26,10},{19,3},{27,11},{20,4},{... | collective-permute-start | bytes 786440 | tf_op jit(solution)/shard_map/ppermute | solution.py:294
  338.2 11.1 %collective-permute-start.30 = (f32[128]{0:T(128)S(1)}, f32[128]{0:T(128)S(1)}, u32[]{:S(2)}, u32[]{:S(2)}) collective-permute-start(f32[128]{0:T(128)S(1)} %fusion.131), channel_id=1, source_target_pairs={{0,8},{8,0},{16,24},{24,16},{1,9},{9,1},{17,25},{25,17},{2,10},{10... | collective-permute-start | bytes 1544 | tf_op jit(solution)/shard_map/ppermute | solution.py:62
  343.6 9.1 %collective-permute-start.32 = (f32[128]{0:T(128)S(1)}, f32[128]{0:T(128)S(1)}, u32[]{:S(2)}, u32[]{:S(2)}) collective-permute-start(f32[128]{0:T(128)S(1)} %fusion.131), channel_id=1, source_target_pairs={{16,8},{24,0},{17,9},{25,1},{18,10},{26,2},{19,11},{27,3},{20,12},... | collective-permute-start | bytes 1544 | tf_op jit(solution)/shard_map/ppermute | solution.py:311
  345.2 7.6 %collective-permute-start.31 = (f32[128]{0:T(128)S(1)}, f32[128]{0:T(128)S(1)}, u32[]{:S(2)}, u32[]{:S(2)}) collective-permute-start(f32[128]{0:T(128)S(1)} %fusion.131), channel_id=1, source_target_pairs={{16,0},{24,8},{17,1},{25,9},{18,2},{26,10},{19,3},{27,11},{20,4},{... | collective-permute-start | bytes 1544 | tf_op jit(solution)/shard_map/ppermute | solution.py:310
  (73 other events, 495.4 us)

commit v2 on v1

--- a/solution.py
+++ b/solution.py
@@ -9,7 +9,7 @@
 
 MASKED_SCORE = -1e30
 EPSILON = 1e-05
-CHUNKS = 4
+CHUNKS = 2
 LOADS = 2
 
 
@@ -222,7 +222,10 @@
         total = times_weight(keep_there, chunk_of(owns, chunk)) + times_weight(
             partner_there, chunk_of(partner_weight, chunk)
         )
-        sent.append(swap(total.astype(jnp.bfloat16), "tensor", 2))
+        total = total.astype(jnp.bfloat16)
+        if chunk:
+            total, sent[chunk - 1] = tied(total, sent[chunk - 1])
+        sent.append(swap(total, "tensor", 2))
     for chunk in range(CHUNKS):
         local.append(
             times_weight(keep_here, chunk_of(owns, chunk))
@@ -240,8 +243,8 @@
     odd = lax.axis_index("section") % 2 == 1
 
     def of_chunk(rows, chunk):
-        parts = rows.reshape(rows.shape[0], samples, CHUNKS, piece)
-        return parts[:, :, chunk].reshape(rows.shape[0], samples * piece)
+        starts = [part * share + chunk * piece for part in range(samples)]
+        return jnp.concatenate([rows[:, start : start + piece] for start in starts], axis=1)
 
     def to_samples(chunk, arrived):
         normed = local[chunk] + arrived.astype(jnp.float32)

time: 366 us -> 323 us (0.88); the launches traced: 360 us -> 321 us
  other arithmetic: 59.5 us -> 40.3 us
  starting transfers between devices: 50 us -> 36.3 us
  local copies, waits for them, and re-layouts: 84.1 us -> 71.3 us
  waiting for transfers between devices: 115 us -> 127 us
  matrix products: 49.6 us -> 44.2 us
    all_to_all x1, waiting for transfers between devices: 0.01 us -> 20.6 us  [on_device(): lax.all_to_all(reduced, 'tensor', split_axis=0, concat_axis=2, tiled=True)]
    ppermute x22 -> x16, waiting for transfers between devices: 101 us -> 85.3 us  [swap(): return lax.ppermute(value, axis, [(i, i ^ bit) for i in range(count)])]
    unnamed x167 -> x131, local copies, waits for them, and re-layouts: 38.3 us -> 25.6 us
    ppermute x4 -> x2, waiting for transfers between devices: 13.5 us -> 19.8 us  [on_device(): at_across[chunk] = lax.ppermute(part, 'section', [(2, 0), (3, 1)])]
    dot_general x16 -> x8, matrix products: 27.9 us -> 21.6 us  [times_weight(): lax.dot_general(rows, weight, (((last - 1, last), (1, 2)), ((), ())), pre...]
    ppermute x22 -> x16, starting transfers between devices: 21.8 us -> 15.9 us  [swap(): return lax.ppermute(value, axis, [(i, i ^ bit) for i in range(count)])]
    concatenate x5 -> x0, local copies, waits for them, and re-layouts: 5.72 us -> none  [the longest x4 5.68 us: whole_chunk(): jnp.concatenate([mine, arrived], axis=1)]
    concatenate x4 -> x2, other arithmetic: 5.63 us -> 0.03 us  [of_chunk(): jnp.concatenate([rows[:, start:start + piece] for start in starts], axis=1)]
  transfers between devices with their start and end apart: 35 -> 25, of which waited for: 13 -> 10; matrix products, arithmetic and copies ran while one was open for 42% -> 43% of each run, Pallas kernels for 0% -> 0%
where the time goes in v2:
time: 323 us; the launch traced here: 321 us
  waiting for transfers between devices  127 us (39%)
  local copies, waits for them, and re-layouts  71.3 us (22%)
  matrix products  44.2 us (14%)
  other arithmetic  40.3 us (12%)
  starting transfers between devices  36.3 us (11%)
    ppermute x16, waiting for transfers between devices, swap(): return lax.ppermute(value, axis, [(i, i ^ bit) for i in range(count)])  85.3 us
    unnamed x131, local copies, waits for them, and re-layouts  25.6 us
    dot_general x8, matrix products, times_weight(): lax.dot_general(rows, weight, (((last - 1, last), (1, 2)), ((), ())), pre...  21.6 us
    all_to_all x1, waiting for transfers between devices, on_device(): lax.all_to_all(reduced, 'tensor', split_axis=0, concat_axis=2, tiled=True)  20.6 us
    ppermute x2, waiting for transfers between devices, on_device(): at_across[chunk] = lax.ppermute(part, 'section', [(2, 0), (3, 1)])  19.8 us
    ppermute x16, starting transfers between devices, swap(): return lax.ppermute(value, axis, [(i, i ^ bit) for i in range(count)])  15.9 us
    sub x2, matrix products, attend_group(): exponent = jnp.exp(scores - row_max)  9.67 us
    dynamic_slice x3, local copies, waits for them, and re-layouts, on_device(): lax.dynamic_slice_in_dim(weight, sample * share + part * load, load, 0)  8.04 us
  transfers between devices with their start and end apart: 25, of which 10 were waited for; matrix products, arithmetic and copies ran while one was open for 43% of the time, Pallas kernels for 0%

profile of v2, /device:TPU:0, one launch (start us, length us, event | category | flops | bytes accessed | tf_op | source)
XLA Modules:
  0.0 321.3 jit_solution(6785028772500811454)
XLA Ops:
  4.6 5.9 %all-to-all-start = ((bf16[2,128,1024]{1,0,2:T(2,128)(2,1)}), bf16[2,128,1024]{1,0,2:T(2,128)(2,1)S(1)}, u32[]{:S(2)}, u32[]{:S(2)}) async-start(bf16[2,128,1024]{1,0,2:T(2,128)(2,1)} %copy.196), calls=%async_computation | async-start | bytes 1048576 | tf_op jit(solution)/shard_map/all_to_all | solution.py:126
  10.5 4.7 %constant_dynamic-slice_fusion.4 = (bf16[1,2048,2,256]{3,2,1,0:T(2,128)(2,1)S(1)}, bf16[1,2048,2,256]{3,2,1,0:T(2,128)(2,1)S(1)}) fusion(bf16[1,8192,2,256]{3,2,1,0:T(2,128)(2,1)} %param.18, s32[]{:T(128)S(6)} %select_n.121, s32[]{:T(128)S(6)} %select_n.125), kind=kLoop, calls=%fused_computation.172 | loop fusion | bytes 8388616 | tf_op jit(solution)/shard_map/dynamic_slice | solution.py:141
  21.5 2.4 bitcast_convert_fusion
  36.9 4.3 %fusion.108 = (f32[128,2048]{1,0:T(8,128)}, f32[128,2048]{1,0:T(8,128)}, f32[128,2048]{1,0:T(8,128)}, f32[128,2048]{1,0:T(8,128)}) fusion(f32[128,8192]{1,0:T(8,128)} %bitcast_convert_fusion), kind=kLoop, calls=%fused_computation.204 | loop fusion | bytes 8388608 | tf_op jit(solution)/shard_map/slice | solution.py:247
  41.2 7.9 %collective-permute-done = bf16[2,512,256]{2,1,0:T(8,128)(2,1)S(1)} collective-permute-done((bf16[2,512,256]{2,1,0:T(8,128)(2,1)}, bf16[2,512,256]{2,1,0:T(8,128)(2,1)S(1)}, u32[]{:S(2)}, u32[]{:S(2)}) %collective-permute-start) | collective-permute-done | bytes 524320 | tf_op jit(solution)/shard_map/ppermute | solution.py:62
  51.4 4.8 %exponential_reduce_fusion.1 = (f32[128,8]{0,1:T(8,128)S(1)}, f32[128,8,1152]{0,2,1:T(8,128)}) fusion(pred[128,1152]{0,1:T(8,128)(4,1)} %pad_add_fusion, bf16[128,2,8,128]{0,3,2,1:T(8,128)(2,1)S(1)} %bitcast.275, bf16[128,128]{1,0:T(8,128)(2,1)S(1)} %copy-done.48, bf16[1024,128]{1,0:T(8,128)(2,1)} %slice.201), kind=kOutput, calls=%fused_computation.19 | convolution fusion | flops 307299456 | bytes 5427200 | tf_op jit(solution)/shard_map/sub | solution.py:37
  56.2 3.1 fusion.41
  72.8 3.0 fusion.52
  75.8 3.6 %collective-permute-done.1 = bf16[1024,256]{0,1:T(8,128)(2,1)} collective-permute-done((bf16[1024,256]{0,1:T(8,128)(2,1)}, bf16[1024,256]{0,1:T(8,128)(2,1)}, u32[]{:S(2)}, u32[]{:S(2)}) %collective-permute-start.1) | collective-permute-done | bytes 524320 | tf_op jit(solution)/shard_map/ppermute | solution.py:62
  82.7 4.9 %exponential_reduce_fusion = (f32[128,8]{0,1:T(8,128)S(1)}, f32[128,8,1152]{0,2,1:T(8,128)}) fusion(pred[128,1152]{0,1:T(8,128)(4,1)} %pad_add_fusion, bf16[128,2,8,128]{0,3,2,1:T(8,128)(2,1)} %bitcast.274, bf16[128,128]{1,0:T(8,128)(2,1)S(1)} %get-tuple-element.112, bf16[1024,128]{1,0:T(8,128)(2,1)} %slice.163), kind=kOutput, calls=%fused_computation.17 | convolution fusion | flops 307299456 | bytes 5427200 | tf_op jit(solution)/shard_map/sub | solution.py:37
  87.6 3.1 fusion.42
  103.9 2.3 fusion.51
  107.1 5.0 %collective-permute-done.4 = bf16[1024,256]{0,1:T(8,128)(2,1)} collective-permute-done((bf16[1024,256]{0,1:T(8,128)(2,1)}, bf16[1024,256]{0,1:T(8,128)(2,1)}, u32[]{:S(2)}, u32[]{:S(2)}) %collective-permute-start.4) | collective-permute-done | bytes 524320 | tf_op jit(solution)/shard_map/ppermute | solution.py:62
  115.6 3.3 %constant_dynamic-slice_fusion = (bf16[2,2,1,128,2,128]{3,2,1,0,5,4:T(2,128)(2,1)}, bf16[2,2,1,128,2,128]{3,2,1,0,5,4:T(2,128)(2,1)}, bf16[2,2,1,128,2,128]{3,2,...) fusion(bf16[2,2,2,128,2,128]{3,2,1,0,5,4:T(2,128)(2,1)S(1)} %convert_element_type.145, s32[]{:T(128)S(6)} %select_n.126, ...), kind=kLoop, calls=%fused_computation.168 | loop fusion | bytes 2097160 | tf_op jit(solution)/shard_map/jit(dynamic_index_in_dim)/dynamic_slice | solution.py:190
  129.3 3.5 %copy.224 = bf16[1,2,2,128,2,256]{5,4,3,2,1,0:T(2,128)(2,1)} copy(bf16[1,2,2,128,2,256]{3,2,1,0,5,4:T(2,128)(2,1)} %pad_maximum_fusion.2) | data formatting | bytes 1048576 | tf_op jit(solution)/shard_map/jit(dynamic_index_in_dim)/dynamic_slice | solution.py:210
  132.8 4.1 %all-to-all-start.1 = ((bf16[512,2,256]{2,1,0:T(2,128)(2,1)}), bf16[512,2,256]{2,1,0:T(2,128)(2,1)}, u32[]{:S(2)}, u32[]{:S(2)}) async-start(bf16[512,2,256]{2,1,0:T(2,128)(2,1)} %bitcast.52), calls=%async_computation.1 | async-start | bytes 1048576 | tf_op jit(solution)/shard_map/all_to_all | solution.py:235
  137.0 2.3 convolution_bitcast_fusion.5
  141.4 3.6 %fusion.15 = bf16[2,128,2048]{2,1,0:T(8,128)(2,1)} fusion(f32[2,128,2048]{2,1,0:T(8,128)S(1)} %convolution_bitcast_fusion.5, bf16[2048,2,256]{2,0,1:T(8,128)(2,1)} %collective-permute-done.2, bf16[2,2,128,2,256]{4,2,3,1,0:T(8,128)(2,1)S(1)} %constant_dynamic-update-slice_fusion, s32[]{:T(128)S(6)} %select_n.124), kind=kOutput, calls=%fused_computation.41 | convolution fusion | flops 537919488 | bytes 5505028 | tf_op jit(solution)/shard_map/dot_general | solution.py:83
  144.9 2.9 collective-permute-start.10
  154.0 20.6 %all-to-all-done.1 = bf16[512,2,256]{2,1,0:T(2,128)(2,1)} async-done(((bf16[512,2,256]{2,1,0:T(2,128)(2,1)}), bf16[512,2,256]{2,1,0:T(2,128)(2,1)}, u32[]{:S(2)}, u32[]{:S(2)}) %all-to-all-start.1) | async-done | bytes 524320 | tf_op jit(solution)/shard_map/all_to_all | solution.py:235
  175.8 4.1 %fusion.16 = bf16[2,128,2048]{2,1,0:T(8,128)(2,1)} fusion(f32[2,128,2048]{2,1,0:T(8,128)} %convolution_bitcast_fusion.7, bf16[2048,2,256]{2,0,1:T(8,128)(2,1)} %collective-permute-done.7, bf16[2,2,128,2,256]{4,2,3,1,0:T(8,128)(2,1)S(1)} %constant_dynamic-update-slice_fusion, s32[]{:T(128)S(6)} %select_n.124), kind=kOutput, calls=%fused_computation.42 | convolution fusion | flops 537919488 | bytes 5505028 | tf_op jit(solution)/shard_map/dot_general | solution.py:83
  179.9 16.2 %collective-permute-done.10 = bf16[2,128,2048]{2,1,0:T(8,128)(2,1)} collective-permute-done((bf16[2,128,2048]{2,1,0:T(8,128)(2,1)}, bf16[2,128,2048]{2,1,0:T(8,128)(2,1)}, u32[]{:S(2)}, u32[]{:S(2)}) %collective-permute-start.10) | collective-permute-done | bytes 1048608 | tf_op jit(solution)/shard_map/ppermute | solution.py:62
  196.0 2.8 fusion.12
  202.7 39.9 %collective-permute-done.11 = bf16[2,128,2048]{2,1,0:T(8,128)(2,1)} collective-permute-done((bf16[2,128,2048]{2,1,0:T(8,128)(2,1)}, bf16[2,128,2048]{2,1,0:T(8,128)(2,1)}, u32[]{:S(2)}, u32[]{:S(2)}) %collective-permute-start.11) | collective-permute-done | bytes 1048608 | tf_op jit(solution)/shard_map/ppermute | solution.py:62
  244.4 2.6 fusion.14
  248.9 12.7 %collective-permute-done.16 = bf16[128,2048]{1,0:T(8,128)(2,1)S(1)} collective-permute-done((bf16[128,2048]{1,0:T(8,128)(2,1)S(1)}, bf16[128,2048]{1,0:T(8,128)(2,1)S(1)}, u32[]{:S(2)}, u32[]{:S(2)}) %collective-permute-start.16) | collective-permute-done | bytes 524320 | tf_op jit(solution)/shard_map/ppermute | solution.py:62
  261.7 2.5 fusion.31
  271.1 2.2 slice_bitcast_fusion.2
  277.4 6.9 %collective-permute-done.14 = bf16[128,2048]{1,0:T(8,128)(2,1)} collective-permute-done((bf16[128,2048]{1,0:T(8,128)(2,1)}, bf16[128,2048]{1,0:T(8,128)(2,1)}, u32[]{:S(2)}, u32[]{:S(2)}) %collective-permute-start.14) | collective-permute-done | bytes 524320 | tf_op jit(solution)/shard_map/ppermute | solution.py:297
  286.3 3.2 fusion.32
  296.1 12.9 %collective-permute-done.18 = bf16[128,2048]{1,0:T(8,128)(2,1)S(1)} collective-permute-done((bf16[128,2048]{1,0:T(8,128)(2,1)S(1)}, bf16[128,2048]{1,0:T(8,128)(2,1)S(1)}, u32[]{:S(2)}, u32[]{:S(2)}) %collective-permute-start.18) | collective-permute-done | bytes 524320 | tf_op jit(solution)/shard_map/ppermute | solution.py:297
  316.2 5.1 %fusion.8 = f32[1,128,8192]{2,1,0:T(8,128)} fusion(f32[128,2048]{1,0:T(8,128)S(1)} %get-tuple-element.95, f32[128,2048]{1,0:T(8,128)S(1)} %get-tuple-element.93, f32[128,2048]{1,0:T(8,128)S(1)} %get-tuple-element.94, f32[128,2048]{1,0:T(8,128)S(1)} %get-tuple-element.92, bf16[128,8192]{1,0:T(8,128)(2,1)} %collective-permute-done.9, ...), kind=kLoop, calls=%fused_computation.21 | loop fusion | flops 15728640 | bytes 16779264 | tf_op jit(solution)/shard_map/broadcast_in_dim | solution.py:333
  (246 shorter events, 113.1 us)
Async XLA Ops:
  0.6 80.6 %collective-permute-start.3 = (bf16[128,8192]{1,0:T(8,128)(2,1)}, bf16[128,8192]{1,0:T(8,128)(2,1)}, u32[]{:S(2)}, u32[]{:S(2)}) collective-permute-start(bf16[128,8192]{1,0:T(8,128)(2,1)} %bitcast.251), channel_id=1, source_target_pairs={{16,0},{24,8},{17,1},{25,9},{18,2},{26,10},{19,3},{27,11},{20,4},{... | collective-permute-start | bytes 6291464 | tf_op jit(solution)/shard_map/ppermute | solution.py:154
  1.9 137.4 %collective-permute-start.8 = (bf16[128,8192]{1,0:T(8,128)(2,1)}, bf16[128,8192]{1,0:T(8,128)(2,1)}, u32[]{:S(2)}, u32[]{:S(2)}) collective-permute-start(bf16[128,8192]{1,0:T(8,128)(2,1)} %bitcast.252), channel_id=1, source_target_pairs={{0,8},{8,0},{16,24},{24,16},{1,9},{9,1},{17,25},{25,17},{2,10},{10... | collective-permute-start | bytes 6291464 | tf_op jit(solution)/shard_map/ppermute | solution.py:62
  4.6 29.6 %all-to-all-start = ((bf16[2,128,1024]{1,0,2:T(2,128)(2,1)}), bf16[2,128,1024]{1,0,2:T(2,128)(2,1)S(1)}, u32[]{:S(2)}, u32[]{:S(2)}) async-start(bf16[2,128,1024]{1,0,2:T(2,128)(2,1)} %copy.196), calls=%async_computation | async-start | bytes 1048576 | tf_op jit(solution)/shard_map/all_to_all | solution.py:126
  17.2 64.1 %collective-permute-start.2 = (bf16[2048,2,256]{2,0,1:T(8,128)(2,1)}, bf16[2048,2,256]{2,0,1:T(8,128)(2,1)}, u32[]{:S(2)}, u32[]{:S(2)}) collective-permute-start(bf16[2048,2,256]{2,0,1:T(8,128)(2,1)} %bitcast.250), channel_id=1, source_target_pairs={{0,1},{1,0},{2,3},{3,2},{4,5},{5,4},{6,7},{7,6},{8,9},{9,8},{10,11... | collective-permute-start | bytes 6291464 | tf_op jit(solution)/shard_map/ppermute | solution.py:62
  20.8 118.5 %collective-permute-start.7 = (bf16[2048,2,256]{2,0,1:T(8,128)(2,1)}, bf16[2048,2,256]{2,0,1:T(8,128)(2,1)}, u32[]{:S(2)}, u32[]{:S(2)}) collective-permute-start(bf16[2048,2,256]{2,0,1:T(8,128)(2,1)} %bitcast.249), channel_id=1, source_target_pairs={{0,1},{1,0},{2,3},{3,2},{4,5},{5,4},{6,7},{7,6},{8,9},{9,8},{10,11... | collective-permute-start | bytes 6291464 | tf_op jit(solution)/shard_map/ppermute | solution.py:62
  26.9 55.8 %copy-start.46 = (bf16[128,128]{1,0:T(8,128)(2,1)}, bf16[128,128]{1,0:T(8,128)(2,1)S(1)}, u32[]{:S(2)}) copy-start(bf16[128,128]{1,0:T(8,128)(2,1)S(1)} %get-tuple-element.112) | copy-start | bytes 98308
  35.4 13.7 %collective-permute-start = (bf16[2,512,256]{2,1,0:T(8,128)(2,1)}, bf16[2,512,256]{2,1,0:T(8,128)(2,1)S(1)}, u32[]{:S(2)}, u32[]{:S(2)}) collective-permute-start(bf16[2,512,256]{2,1,0:T(8,128)(2,1)} %bitcast.272), channel_id=1, source_target_pairs={{0,4},{4,0},{1,5},{5,1},{2,6},{6,2},{3,7},{7,3},{8,12},{12,8},{9,1... | collective-permute-start | bytes 1572872 | tf_op jit(solution)/shard_map/ppermute | solution.py:62
  66.5 13.0 %collective-permute-start.1 = (bf16[1024,256]{0,1:T(8,128)(2,1)}, bf16[1024,256]{0,1:T(8,128)(2,1)}, u32[]{:S(2)}, u32[]{:S(2)}) collective-permute-start(bf16[1024,256]{0,1:T(8,128)(2,1)} %fusion.54), channel_id=1, source_target_pairs={{0,4},{4,0},{1,5},{5,1},{2,6},{6,2},{3,7},{7,3},{8,12},{12,8},{9,1... | collective-permute-start | bytes 1572872 | tf_op jit(solution)/shard_map/ppermute | solution.py:62
  92.7 46.6 %collective-permute-start.9 = (bf16[128,8192]{1,0:T(8,128)(2,1)}, bf16[128,8192]{1,0:T(8,128)(2,1)}, u32[]{:S(2)}, u32[]{:S(2)}) collective-permute-start(bf16[128,8192]{1,0:T(8,128)(2,1)} %collective-permute-done.3), channel_id=1, source_target_pairs={{0,8},{8,0},{16,24},{24,16},{1,9},{9,1},{17,25},{25,17},{2,10},{10... | collective-permute-start | bytes 6291464 | tf_op jit(solution)/shard_map/ppermute | solution.py:62
  97.5 14.6 %collective-permute-start.4 = (bf16[1024,256]{0,1:T(8,128)(2,1)}, bf16[1024,256]{0,1:T(8,128)(2,1)}, u32[]{:S(2)}, u32[]{:S(2)}) collective-permute-start(bf16[1024,256]{0,1:T(8,128)(2,1)} %fusion.53), channel_id=1, source_target_pairs={{0,4},{4,0},{1,5},{5,1},{2,6},{6,2},{3,7},{7,3},{8,12},{12,8},{9,1... | collective-permute-start | bytes 1572872 | tf_op jit(solution)/shard_map/ppermute | solution.py:62
  123.9 15.4 %collective-permute-start.5 = (bf16[2,2,128,2,128]{4,2,3,1,0:T(8,128)(2,1)}, bf16[2,2,128,2,128]{4,2,3,1,0:T(8,128)(2,1)}, u32[]{:S(2)}, u32[]{:S(2)}) collective-permute-start(bf16[2,2,128,2,128]{4,2,3,1,0:T(8,128)(2,1)} %bitcast.286), channel_id=1, source_target_pairs={{0,1},{1,0},{2,3},{3,2},{4,5},{5,4},{6,7},{7,6},{8,9},{9,8},{10,11... | collective-permute-start | bytes 786440 | tf_op jit(solution)/shard_map/ppermute | solution.py:62
  126.5 12.8 %collective-permute-start.6 = (bf16[2,2,128,2,128]{4,2,3,1,0:T(8,128)(2,1)}, bf16[2,2,128,2,128]{4,2,3,1,0:T(8,128)(2,1)}, u32[]{:S(2)}, u32[]{:S(2)}) collective-permute-start(bf16[2,2,128,2,128]{4,2,3,1,0:T(8,128)(2,1)} %bitcast.287), channel_id=1, source_target_pairs={{0,1},{1,0},{2,3},{3,2},{4,5},{5,4},{6,7},{7,6},{8,9},{9,8},{10,11... | collective-permute-start | bytes 786440 | tf_op jit(solution)/shard_map/ppermute | solution.py:62
  132.8 41.8 %all-to-all-start.1 = ((bf16[512,2,256]{2,1,0:T(2,128)(2,1)}), bf16[512,2,256]{2,1,0:T(2,128)(2,1)}, u32[]{:S(2)}, u32[]{:S(2)}) async-start(bf16[512,2,256]{2,1,0:T(2,128)(2,1)} %bitcast.52), calls=%async_computation.1 | async-start | bytes 1048576 | tf_op jit(solution)/shard_map/all_to_all | solution.py:235
  141.4 34.4 %copy-start.25 = (bf16[2,2,128,2,256]{4,2,3,1,0:T(8,128)(2,1)}, bf16[2,2,128,2,256]{4,2,3,1,0:T(8,128)(2,1)S(1)}, u32[]{:S(2)}) copy-start(bf16[2,2,128,2,256]{4,2,3,1,0:T(8,128)(2,1)S(1)} %constant_dynamic-update-slice_fusion) | copy-start | bytes 1572868
  144.9 51.1 %collective-permute-start.10 = (bf16[2,128,2048]{2,1,0:T(8,128)(2,1)}, bf16[2,128,2048]{2,1,0:T(8,128)(2,1)}, u32[]{:S(2)}, u32[]{:S(2)}) collective-permute-start(bf16[2,128,2048]{2,1,0:T(8,128)(2,1)} %fusion.15), channel_id=1, source_target_pairs={{0,2},{1,3},{2,0},{3,1},{4,6},{5,7},{6,4},{7,5},{8,10},{9,11},{10,... | collective-permute-start | bytes 3145736 | tf_op jit(solution)/shard_map/ppermute | solution.py:62
  175.8 20.3 %copy-start.8 = (f32[2,128,2048]{2,1,0:T(8,128)S(1)}, f32[2,128,2048]{2,1,0:T(8,128)}, u32[]{:S(2)}) copy-start(f32[2,128,2048]{2,1,0:T(8,128)} %convolution_bitcast_fusion.3) | copy-start | bytes 6291460
  196.0 46.6 %collective-permute-start.11 = (bf16[2,128,2048]{2,1,0:T(8,128)(2,1)}, bf16[2,128,2048]{2,1,0:T(8,128)(2,1)}, u32[]{:S(2)}, u32[]{:S(2)}) collective-permute-start(bf16[2,128,2048]{2,1,0:T(8,128)(2,1)} %fusion.16), channel_id=1, source_target_pairs={{0,2},{1,3},{2,0},{3,1},{4,6},{5,7},{6,4},{7,5},{8,10},{9,11},{10,... | collective-permute-start | bytes 3145736 | tf_op jit(solution)/shard_map/ppermute | solution.py:62
  199.7 43.0 %collective-permute-start.12 = (bf16[128,2048]{1,0:T(8,128)(2,1)}, bf16[128,2048]{1,0:T(8,128)(2,1)}, u32[]{:S(2)}, u32[]{:S(2)}) collective-permute-start(bf16[128,2048]{1,0:T(8,128)(2,1)} %fusion.57), channel_id=1, source_target_pairs={{0,4},{4,0},{1,5},{5,1},{2,6},{6,2},{3,7},{7,3},{8,12},{12,8},{9,1... | collective-permute-start | bytes 1572872 | tf_op jit(solution)/shard_map/ppermute | solution.py:62
  202.6 41.3 %copy-start.52 = (f32[128]{0:T(128)S(1)}, f32[128]{0:T(128)}, u32[]{:S(2)}) copy-start(f32[128]{0:T(128)} %add_rsqrt_fusion) | copy-start | bytes 1540
  244.3 17.3 %collective-permute-start.13 = (bf16[128,4096]{1,0:T(8,128)(2,1)S(1)}, bf16[128,4096]{1,0:T(8,128)(2,1)S(1)}, u32[]{:S(2)}, u32[]{:S(2)}) collective-permute-start(bf16[128,4096]{1,0:T(8,128)(2,1)S(1)} %multiply_convert_fusion.1), channel_id=1, source_target_pairs={{0,8},{8,0},{16,24},{24,16},{1,9},{9,1},{17,25},{25,17},{2,10},{10... | collective-permute-start | bytes 3145736 | tf_op jit(solution)/shard_map/ppermute | solution.py:62
  247.1 14.5 %copy-start.23 = (f32[128,2048]{1,0:T(8,128)S(1)}, f32[128,2048]{1,0:T(8,128)}, u32[]{:S(2)}) copy-start(f32[128,2048]{1,0:T(8,128)} %get-tuple-element.85) | copy-start | bytes 3145732
  247.2 14.5 %copy-start.24 = (f32[128,2048]{1,0:T(8,128)S(1)}, f32[128,2048]{1,0:T(8,128)}, u32[]{:S(2)}) copy-start(f32[128,2048]{1,0:T(8,128)} %get-tuple-element.86) | copy-start | bytes 3145732
  247.2 14.4 %collective-permute-start.16 = (bf16[128,2048]{1,0:T(8,128)(2,1)S(1)}, bf16[128,2048]{1,0:T(8,128)(2,1)S(1)}, u32[]{:S(2)}, u32[]{:S(2)}) collective-permute-start(bf16[128,2048]{1,0:T(8,128)(2,1)S(1)} %fusion.58), channel_id=1, source_target_pairs={{0,4},{4,0},{1,5},{5,1},{2,6},{6,2},{3,7},{7,3},{8,12},{12,8},{9,1... | collective-permute-start | bytes 1572872 | tf_op jit(solution)/shard_map/ppermute | solution.py:62
  264.2 22.1 %collective-permute-start.17 = (bf16[128,4096]{1,0:T(8,128)(2,1)}, bf16[128,4096]{1,0:T(8,128)(2,1)}, u32[]{:S(2)}, u32[]{:S(2)}) collective-permute-start(bf16[128,4096]{1,0:T(8,128)(2,1)} %get-tuple-element.118), channel_id=1, source_target_pairs={{0,8},{8,0},{16,24},{24,16},{1,9},{9,1},{17,25},{25,17},{2,10},{10... | collective-permute-start | bytes 3145736 | tf_op jit(solution)/shard_map/ppermute | solution.py:62
  266.3 18.1 %collective-permute-start.14 = (bf16[128,2048]{1,0:T(8,128)(2,1)}, bf16[128,2048]{1,0:T(8,128)(2,1)}, u32[]{:S(2)}, u32[]{:S(2)}) collective-permute-start(bf16[128,2048]{1,0:T(8,128)(2,1)} %slice_select_fusion.1), channel_id=1, source_target_pairs={{16,0},{24,8},{17,1},{25,9},{18,2},{26,10},{19,3},{27,11},{20,4},{... | collective-permute-start | bytes 1572872 | tf_op jit(solution)/shard_map/ppermute | solution.py:297
  284.4 9.8 %collective-permute-start.15 = (bf16[128,2048]{1,0:T(8,128)(2,1)}, bf16[128,2048]{1,0:T(8,128)(2,1)S(1)}, u32[]{:S(2)}, u32[]{:S(2)}) collective-permute-start(bf16[128,2048]{1,0:T(8,128)(2,1)} %collective-permute-done.14), channel_id=1, source_target_pairs={{0,8},{8,0},{1,9},{9,1},{2,10},{10,2},{3,11},{11,3},{4,12},{12,4},... | collective-permute-start | bytes 1572872 | tf_op jit(solution)/shard_map/ppermute | solution.py:290
  289.5 25.3 %collective-permute-start.22 = (f32[128]{0:T(128)S(1)}, f32[128]{0:T(128)S(1)}, u32[]{:S(2)}, u32[]{:S(2)}) collective-permute-start(f32[128]{0:T(128)S(1)} %fusion.82), channel_id=1, source_target_pairs={{16,8},{24,0},{17,9},{25,1},{18,10},{26,2},{19,11},{27,3},{20,12},... | collective-permute-start | bytes 1544 | tf_op jit(solution)/shard_map/ppermute | solution.py:314
  290.9 23.9 %collective-permute-start.21 = (f32[128]{0:T(128)S(1)}, f32[128]{0:T(128)S(1)}, u32[]{:S(2)}, u32[]{:S(2)}) collective-permute-start(f32[128]{0:T(128)S(1)} %fusion.82), channel_id=1, source_target_pairs={{16,0},{24,8},{17,1},{25,9},{18,2},{26,10},{19,3},{27,11},{20,4},{... | collective-permute-start | bytes 1544 | tf_op jit(solution)/shard_map/ppermute | solution.py:313
  292.2 18.8 %collective-permute-start.20 = (f32[128]{0:T(128)S(1)}, f32[128]{0:T(128)S(1)}, u32[]{:S(2)}, u32[]{:S(2)}) collective-permute-start(f32[128]{0:T(128)S(1)} %fusion.82), channel_id=1, source_target_pairs={{0,8},{8,0},{16,24},{24,16},{1,9},{9,1},{17,25},{25,17},{2,10},{10... | collective-permute-start | bytes 1544 | tf_op jit(solution)/shard_map/ppermute | solution.py:62
  292.9 16.1 %collective-permute-start.18 = (bf16[128,2048]{1,0:T(8,128)(2,1)S(1)}, bf16[128,2048]{1,0:T(8,128)(2,1)S(1)}, u32[]{:S(2)}, u32[]{:S(2)}) collective-permute-start(bf16[128,2048]{1,0:T(8,128)(2,1)S(1)} %slice_select_fusion), channel_id=1, source_target_pairs={{16,0},{24,8},{17,1},{25,9},{18,2},{26,10},{19,3},{27,11},{20,4},{... | collective-permute-start | bytes 1572872 | tf_op jit(solution)/shard_map/ppermute | solution.py:297
  296.1 16.7 %copy-start.6 = (f32[128,2048]{1,0:T(8,128)S(1)}, f32[128,2048]{1,0:T(8,128)}, u32[]{:S(2)}) copy-start(f32[128,2048]{1,0:T(8,128)} %copy-done.5) | copy-start | bytes 3145732
  309.0 3.8 %collective-permute-start.19 = (bf16[128,2048]{1,0:T(8,128)(2,1)S(1)}, bf16[128,2048]{1,0:T(8,128)(2,1)S(1)}, u32[]{:S(2)}, u32[]{:S(2)}) collective-permute-start(bf16[128,2048]{1,0:T(8,128)(2,1)S(1)} %collective-permute-done.18), channel_id=1, source_target_pairs={{0,8},{8,0},{1,9},{9,1},{2,10},{10,2},{3,11},{11,3},{4,12},{12,4},... | collective-permute-start | bytes 1572872 | tf_op jit(solution)/shard_map/ppermute | solution.py:290
  (52 other events, 214.2 us)
